TPU v7x, 128 devices: a whole 4x4x4 slice. The times are simulated.
128 devices in a mesh: group: 4 (over y), sub: 32 (over x, z, core).
Axes of the slice: x: 4, y: 4, z: 4, core: 2. Of those that a mesh axis runs over, the one named last changes fastest.
Arguments:
- adjoint_start: float32 [6, 128, 12288], P(None, 'group', 'sub'), may hold values from -6 to 6
- objective_grad: float32 [6, 128, 12288], P(None, 'group', 'sub'), may hold values from -24 to 24
- diagonal: float32 [128, 12288], P('group', 'sub'), may hold values from 4 to 8
- connect: int32 [64, 43264], P(None, ('group', 'sub')), may hold values from 0 to 14819, as said below
- element_scale: float32 [64, 43264], P(None, ('group', 'sub')), may hold values from 0.5 to 2
- element_matrix: bfloat16 [64, 64], replicated, may hold values from -0.75 to 0.75
- traction_map: float32 [3, 6], replicated, may hold values from -2.5 to 2.5
- iface_node: int32 [262144], P(('group', 'sub')), may hold values from 0 to 12287
- iface_dest: int32 [262144, 1], P(('group', 'sub')), may hold values from 0 to 127; in each aligned block of 2048 rows (0 to 2047, 2048 to 4095, ...) at most 32 rows name the same one
- iface_target: int32 [262144], P(('group', 'sub')), may hold values from 0 to 2047
- iface_count: int32 [128], P(('group', 'sub')), may hold values from 1 to 2048, 196608 in all
Outputs:
- adjoint: float32 [6, 128, 12288], P(None, 'group', 'sub')
- struct_load: float32 [2, 3, 262144], P(None, None, ('group', 'sub'))
Inputs may be any that keep to these rules, and one draw needn't show every extreme that they name: `connect`: the elements of one device tile its extended grid in an order drawn from the seed: element nodes are 4 consecutive rows by 16 consecutive columns, starting at row min(3 i, 34) and column min(15 j, 374) for every i below (36) // 3 + 1 and j below (388) // 15 + 1, each such element once. `iface_dest`: among the rows of one device, no structural device is named by more than 32 rows.
All inputs are finite; a program needn't handle non-finite values. No bound on the sum of `iface_count` on one device may be relied on, other than what follows from the above.
Results may differ from a plain program's by a relative error of at most 0.00091.
Values sent between devices are 32-bit elements; how exact they have to be, the bound alone decides.
A program may use at most 128 MiB of HBM per device.

v0:
```python
import jax
import jax.numpy as jnp
from jax import lax
from jax.sharding import PartitionSpec as P

COMP = 6
SPAN_DEV = 32
CROSS_DEV = 384
IF_CAP = 2048
S_DEV = 2048
ITERS = 2
SWEEPS = 2


def with_halo(value, sides, width):
    for axis, dim in sides:
        size, length = (lax.axis_size(axis), value.shape[dim])
        up = [(i, (i + 1) % size) for i in range(size - 1)]
        down = [(j, i) for i, j in up]
        last = lax.slice_in_dim(value, length - width, length, axis=dim)
        leading = lax.slice_in_dim(value, 0, width, axis=dim)
        before = lax.ppermute(last, axis, up)
        after = lax.ppermute(leading, axis, down)
        value = jnp.concatenate([before, value, after], axis=dim)
    return value


def element_terms(source, conn_part, scale_part, target_part, element_matrix, own_nodes):
    count = conn_part.shape[1]
    gathered = jnp.take(source, conn_part.reshape(-1), axis=1).reshape(COMP, 64, count)
    scaled = (gathered * scale_part[None]).astype(jnp.bfloat16)
    elem_out = jnp.einsum("cje,jk->cke", scaled, element_matrix, preferred_element_type=jnp.float32)
    elem_out = elem_out.reshape(COMP, 64 * count)
    summed = jax.vmap(lambda values: jax.ops.segment_sum(values, target_part, own_nodes + 1))(
        elem_out
    )
    return summed[:, :own_nodes]


def on_device(
    adjoint_start,
    objective_grad,
    diagonal,
    connect,
    element_scale,
    element_matrix,
    traction_map,
    iface_node,
    iface_dest,
    iface_target,
    iface_count,
):
    groups = lax.axis_size("group")
    subs = lax.axis_size("sub")
    devices = groups * subs
    cap = max(2, 2 * IF_CAP // devices)
    ext_cols = CROSS_DEV + 6
    own_nodes = SPAN_DEV * CROSS_DEV
    row_ext = connect // ext_cols
    col_ext = connect % ext_cols
    inside = (row_ext >= 3) & (row_ext < SPAN_DEV + 3) & (col_ext >= 3) & (col_ext < CROSS_DEV + 3)
    target_own = jnp.where(inside, (row_ext - 3) * CROSS_DEV + col_ext - 3, own_nodes)
    target_flat = target_own.reshape(-1)
    dest_row = iface_dest[:, 0]
    live = jnp.arange(IF_CAP, dtype=jnp.int32) < iface_count[0]
    onehot = (
        (dest_row[:, None] == jnp.arange(devices, dtype=jnp.int32)[None, :]) & live[:, None]
    ).astype(jnp.int32)
    before = jnp.cumsum(onehot, axis=0) - onehot
    slot_of = jnp.sum(before * onehot, axis=1)
    position = jnp.where(live, dest_row * cap + slot_of, devices * cap)
    target_buffer = jnp.zeros((devices * cap + 1,), jnp.int32).at[position].set(iface_target)
    target_buffer = target_buffer[: devices * cap]
    adjoint = adjoint_start
    loads = []
    for outer in range(ITERS):
        for inner in range(SWEEPS):
            extended = with_halo(adjoint, (("group", 1), ("sub", 2)), 3)
            extended = extended.reshape(COMP, -1)
            summed = element_terms(
                extended, connect, element_scale, target_flat, element_matrix, own_nodes
            )
            assembled = summed.reshape(COMP, SPAN_DEV, CROSS_DEV)
            adjoint = (objective_grad - assembled) / diagonal[None]
        values = jnp.take(adjoint.reshape(COMP, own_nodes), iface_node, axis=1)
        traction = jnp.dot(traction_map, values, precision=lax.Precision.HIGHEST)
        traction = jnp.where(live[None, :], traction, 0.0)
        buffer = jnp.zeros((devices * cap + 1, 3), jnp.float32).at[position].set(traction.T)
        buffer = buffer[: devices * cap]
        moved = lax.all_to_all(
            buffer.reshape(devices, cap, 3),
            ("group", "sub"),
            split_axis=0,
            concat_axis=0,
            tiled=True,
        )
        names = lax.all_to_all(
            target_buffer.reshape(devices, cap),
            ("group", "sub"),
            split_axis=0,
            concat_axis=0,
            tiled=True,
        )
        load = jax.ops.segment_sum(moved.reshape(-1, 3), names.reshape(-1), S_DEV)
        loads.append(load.T)
    return (adjoint, jnp.stack(loads))


def solution(mesh):
    placed = (
        P(None, "group", "sub"),
        P(None, "group", "sub"),
        P("group", "sub"),
        P(None, ("group", "sub")),
        P(None, ("group", "sub")),
        P(),
        P(),
        P(("group", "sub")),
        P(("group", "sub"), None),
        P(("group", "sub")),
        P(("group", "sub")),
    )
    return jax.shard_map(
        on_device,
        mesh=mesh,
        in_specs=placed,
        out_specs=(P(None, "group", "sub"), P(None, None, ("group", "sub"))),
        check_vma=False,
    )
```

profile of v0, /device:TPU:1, one launch (start us, length us, event | category | flops | bytes accessed | tf_op | source)
XLA Modules:
  0.0 1003.3 jit_solution(11820166655426375882)
XLA Ops:
  29.8 43.8 %gather_fusion = f32[21632,6]{1,0:T(8,128)} fusion(f32[6,14820]{0,1:T(8,128)} %copy.70, s32[22528]{0:T(1024)S(1)} %pad_clamp_fusion), kind=kCustom, calls=%fused_computation.clone | custom fusion | bytes 1124864 | tf_op jit(solution)/shard_map/jit(_take)/gather | solution.py:30
  73.6 13.1 %select_bitcast_fusion.3 = f32[6,21632]{0,1:T(8,128)} fusion(f32[21632,6]{1,0:T(8,128)} %gather_fusion, pred[21632]{0:T(1024)(128)(4,1)S(1)} %compare_and_fusion), kind=kLoop, calls=%fused_computation.26 | loop fusion | flops 129792 | bytes 1059968 | tf_op jit(solution)/shard_map/jit(_take)/select_n | solution.py:30
  86.8 6.9 copy.71
  101.4 110.3 %scatter_custom_fusion = f32[6,12289]{0,1:T(8,128)} fusion(s32[21632]{0:T(1024)S(1)} %reshape.228, f32[6,21632]{0,1:T(8,128)} %copy.73, f32[]{:T(128)} %constant.31.clone.1), kind=kCustom, calls=%fused_computation.21 | custom fusion | flops 129792 | bytes 814108 | tf_op jit(solution)/shard_map/vmap()/scatter-add | solution.py:34
  245.1 43.8 %gather_fusion.1 = f32[21632,6]{1,0:T(8,128)} fusion(f32[6,14820]{0,1:T(8,128)} %copy.75, s32[22528]{0:T(1024)S(1)} %pad_clamp_fusion), kind=kCustom, calls=%fused_computation.2.clone | custom fusion | bytes 1124864 | tf_op jit(solution)/shard_map/jit(_take)/gather | solution.py:30
  288.9 13.1 %select_bitcast_fusion.2 = f32[6,21632]{0,1:T(8,128)} fusion(f32[21632,6]{1,0:T(8,128)} %gather_fusion.1, pred[21632]{0:T(1024)(128)(4,1)S(1)} %compare_and_fusion), kind=kLoop, calls=%fused_computation.25 | loop fusion | flops 129792 | bytes 1059968 | tf_op jit(solution)/shard_map/jit(_take)/select_n | solution.py:30
  302.0 6.9 copy.76
  318.5 110.3 %scatter_custom_fusion.1 = f32[6,12289]{0,1:T(8,128)} fusion(s32[21632]{0:T(1024)S(1)} %reshape.228, f32[6,21632]{0,1:T(8,128)} %copy.78, f32[]{:T(128)} %constant.31.clone.1), kind=kCustom, calls=%fused_computation.19 | custom fusion | flops 129792 | bytes 814108 | tf_op jit(solution)/shard_map/vmap()/scatter-add | solution.py:34
  451.3 8.2 scatter_custom_fusion.4
  460.2 12.0 %all-to-all-start = ((s32[128,1,32]{2,1,0:T(1,128)}), s32[128,1,32]{2,1,0:T(1,128)}, u32[]{:S(2)}, u32[]{:S(2)}) async-start(s32[128,1,32]{2,1,0:T(1,128)} %bitcast.28), calls=%async_computation | async-start | bytes 131072 | tf_op jit(solution)/shard_map/all_to_all | solution.py:97
  478.0 43.9 %gather_fusion.2 = f32[21632,6]{1,0:T(8,128)} fusion(f32[6,14820]{0,1:T(8,128)} %copy.80, s32[22528]{0:T(1024)S(1)} %pad_clamp_fusion), kind=kCustom, calls=%fused_computation.3.clone | custom fusion | bytes 1124864 | tf_op jit(solution)/shard_map/jit(_take)/gather | solution.py:30
  521.9 13.1 %select_bitcast_fusion.1 = f32[6,21632]{0,1:T(8,128)} fusion(f32[21632,6]{1,0:T(8,128)} %gather_fusion.2, pred[21632]{0:T(1024)(128)(4,1)S(1)} %compare_and_fusion), kind=kLoop, calls=%fused_computation.24 | loop fusion | flops 129792 | bytes 1059968 | tf_op jit(solution)/shard_map/jit(_take)/select_n | solution.py:30
  535.1 6.9 copy.81
  549.6 110.3 %scatter_custom_fusion.2 = f32[6,12289]{0,1:T(8,128)} fusion(s32[21632]{0:T(1024)S(1)} %reshape.228, f32[6,21632]{0,1:T(8,128)} %copy.83, f32[]{:T(128)} %constant.31.clone.1), kind=kCustom, calls=%fused_computation.17 | custom fusion | flops 129792 | bytes 814108 | tf_op jit(solution)/shard_map/vmap()/scatter-add | solution.py:34
  678.0 8.2 gather_fusion.4
  712.5 44.0 %gather_fusion.3 = f32[21632,6]{1,0:T(8,128)} fusion(f32[6,14820]{0,1:T(8,128)} %copy.85, s32[22528]{0:T(1024)S(1)} %pad_clamp_fusion), kind=kCustom, calls=%fused_computation.4.clone | custom fusion | bytes 1124864 | tf_op jit(solution)/shard_map/jit(_take)/gather | solution.py:30
  756.5 13.1 %select_bitcast_fusion = f32[6,21632]{0,1:T(8,128)} fusion(f32[21632,6]{1,0:T(8,128)} %gather_fusion.3, pred[21632]{0:T(1024)(128)(4,1)S(1)} %compare_and_fusion), kind=kLoop, calls=%fused_computation.23 | loop fusion | flops 129792 | bytes 1059968 | tf_op jit(solution)/shard_map/jit(_take)/select_n | solution.py:30
  769.6 6.9 copy.86
  784.2 110.2 %scatter_custom_fusion.3 = f32[6,12289]{0,1:T(8,128)} fusion(s32[21632]{0:T(1024)} %copy-done.6, f32[6,21632]{0,1:T(8,128)} %copy.88, f32[]{:T(128)} %constant.31.clone.1), kind=kCustom, calls=%fused_computation.15 | custom fusion | flops 129792 | bytes 11371032 | tf_op jit(solution)/shard_map/vmap()/scatter-add | solution.py:34
  907.8 8.2 gather_fusion.5
  916.1 11.2 %all-to-all-start.1 = ((f32[128,32,3]{1,2,0:T(4,128)}), f32[128,32,3]{1,2,0:T(4,128)S(1)}, u32[]{:S(2)}, u32[]{:S(2)}) async-start(f32[128,32,3]{1,2,0:T(4,128)} %copy.96), calls=%async_computation.1 | async-start | bytes 524288 | tf_op jit(solution)/shard_map/all_to_all | solution.py:90
  940.9 9.8 all-to-all-start.2
  954.7 23.0 %scatter_custom_fusion.6 = f32[2048,3]{1,0:T(8,128)S(1)} fusion(s32[4096]{0:T(1024)S(1)} %reshape.252, f32[4096,3]{1,0:T(8,128)S(1)} %bitcast.97, f32[]{:T(128)} %constant.31.clone.1), kind=kCustom, calls=%fused_computation.60 | custom fusion | flops 12288 | bytes 24580 | tf_op jit(solution)/shard_map/scatter-add | solution.py:104
  978.9 23.0 %scatter_custom_fusion.8 = f32[2048,3]{1,0:T(8,128)S(1)} fusion(s32[4096]{0:T(1024)S(1)} %reshape.252, f32[4096,3]{1,0:T(8,128)S(1)} %bitcast.96, f32[]{:T(128)} %constant.31.clone.1), kind=kCustom, calls=%fused_computation.58 | custom fusion | flops 12288 | bytes 24580 | tf_op jit(solution)/shard_map/scatter-add | solution.py:104
  (146 shorter events, 200.5 us)
Async XLA Ops:
  0.6 93.7 %copy-start = (bf16[64,64]{1,0:T(8,128)(2,1)S(1)}, bf16[64,64]{1,0:T(8,128)(2,1)}, u32[]{:S(2)}) copy-start(bf16[64,64]{1,0:T(8,128)(2,1)} %param.20) | copy-start | bytes 24580
  1.6 9.6 collective-permute-start
  5.6 5.6 collective-permute-start.1
  12.3 6.8 collective-permute-start.2
  16.9 6.2 collective-permute-start.3
  19.1 530.5 %copy-start.6 = (s32[21632]{0:T(1024)}, s32[21632]{0:T(1024)S(1)}, u32[]{:S(2)}) copy-start(s32[21632]{0:T(1024)S(1)} %reshape.228) | copy-start | bytes 259588
  19.1 54.5 %copy-start.8 = (s32[128,17]{0,1:T(8,128)}, s32[128,17]{0,1:T(8,128)S(1)}, u32[]{:S(2)}) copy-start(s32[128,17]{0,1:T(8,128)S(1)} %reduce-window.9) | copy-start | bytes 26116
  221.0 5.4 collective-permute-start.4
  225.1 4.7 collective-permute-start.5
  229.9 6.0 collective-permute-start.6
  233.2 6.2 collective-permute-start.7
  438.0 5.7 collective-permute-start.8
  441.3 4.7 collective-permute-start.9
  446.1 26.2 %collective-permute-start.10 = (f32[6,38,3]{2,1,0:T(8,128)S(1)}, f32[6,38,3]{2,1,0:T(8,128)S(1)}, u32[]{:S(2)}, u32[]{:S(2)}) collective-permute-start(f32[6,38,3]{2,1,0:T(8,128)S(1)} %get-tuple-element.10), channel_id=1, source_target_pairs={{0,1},{1,2},{2,3},{3,4},{4,5},{5,6},{6,7},{7,8},{8,9},{9,10},{10,1... | collective-permute-start | bytes 8216 | tf_op jit(solution)/shard_map/ppermute | solution.py:22
  449.3 23.0 %collective-permute-start.11 = (f32[6,38,3]{2,1,0:T(8,128)S(1)}, f32[6,38,3]{2,1,0:T(8,128)S(1)}, u32[]{:S(2)}, u32[]{:S(2)}) collective-permute-start(f32[6,38,3]{2,1,0:T(8,128)S(1)} %get-tuple-element.11), channel_id=1, source_target_pairs={{1,0},{2,1},{3,2},{4,3},{5,4},{6,5},{7,6},{8,7},{9,8},{10,9},{11,1... | collective-permute-start | bytes 8216 | tf_op jit(solution)/shard_map/ppermute | solution.py:23
  460.2 455.8 %all-to-all-start = ((s32[128,1,32]{2,1,0:T(1,128)}), s32[128,1,32]{2,1,0:T(1,128)}, u32[]{:S(2)}, u32[]{:S(2)}) async-start(s32[128,1,32]{2,1,0:T(1,128)} %bitcast.28), calls=%async_computation | async-start | bytes 131072 | tf_op jit(solution)/shard_map/all_to_all | solution.py:97
  664.6 27.5 %copy-start.10 = (f32[3,6]{1,0:T(4,128)S(1)}, f32[3,6]{1,0:T(4,128)}, u32[]{:S(2)}) copy-start(f32[3,6]{1,0:T(4,128)} %param.21) | copy-start | bytes 220
  669.2 17.0 %collective-permute-start.12 = (f32[6,3,384]{2,1,0:T(4,128)S(1)}, f32[6,3,384]{2,1,0:T(4,128)S(1)}, u32[]{:S(2)}, u32[]{:S(2)}) collective-permute-start(f32[6,3,384]{2,1,0:T(4,128)S(1)} %get-tuple-element.16), channel_id=1, source_target_pairs={{0,32},{32,64},{64,96},{1,33},{33,65},{65,97},{2,34},{34,66},{66,9... | collective-permute-start | bytes 82952 | tf_op jit(solution)/shard_map/ppermute | solution.py:22
  672.5 13.7 %collective-permute-start.13 = (f32[6,3,384]{2,1,0:T(4,128)S(1)}, f32[6,3,384]{2,1,0:T(4,128)S(1)}, u32[]{:S(2)}, u32[]{:S(2)}) collective-permute-start(f32[6,3,384]{2,1,0:T(4,128)S(1)} %get-tuple-element.17), channel_id=1, source_target_pairs={{32,0},{64,32},{96,64},{33,1},{65,33},{97,65},{34,2},{66,34},{98,6... | collective-permute-start | bytes 82952 | tf_op jit(solution)/shard_map/ppermute | solution.py:23
  686.4 19.5 %collective-permute-start.14 = (f32[6,38,3]{2,1,0:T(8,128)S(1)}, f32[6,38,3]{2,1,0:T(8,128)S(1)}, u32[]{:S(2)}, u32[]{:S(2)}) collective-permute-start(f32[6,38,3]{2,1,0:T(8,128)S(1)} %get-tuple-element.8), channel_id=1, source_target_pairs={{0,1},{1,2},{2,3},{3,4},{4,5},{5,6},{6,7},{7,8},{8,9},{9,10},{10,1... | collective-permute-start | bytes 8216 | tf_op jit(solution)/shard_map/ppermute | solution.py:22
  690.2 15.7 %collective-permute-start.15 = (f32[6,38,3]{2,1,0:T(8,128)S(1)}, f32[6,38,3]{2,1,0:T(8,128)}, u32[]{:S(2)}, u32[]{:S(2)}) collective-permute-start(f32[6,38,3]{2,1,0:T(8,128)S(1)} %get-tuple-element.9), channel_id=1, source_target_pairs={{1,0},{2,1},{3,2},{4,3},{5,4},{6,5},{7,6},{8,7},{9,8},{10,9},{11,1... | collective-permute-start | bytes 8216 | tf_op jit(solution)/shard_map/ppermute | solution.py:23
  903.7 34.1 %copy-start.3 = (f32[6,32,384]{2,1,0:T(8,128)}, f32[6,32,384]{2,1,0:T(8,128)S(1)}, u32[]{:S(2)}) copy-start(f32[6,32,384]{2,1,0:T(8,128)S(1)} %subtract_divide_fusion) | copy-start | bytes 884740
  916.1 24.8 %all-to-all-start.1 = ((f32[128,32,3]{1,2,0:T(4,128)}), f32[128,32,3]{1,2,0:T(4,128)S(1)}, u32[]{:S(2)}, u32[]{:S(2)}) async-start(f32[128,32,3]{1,2,0:T(4,128)} %copy.96), calls=%async_computation.1 | async-start | bytes 524288 | tf_op jit(solution)/shard_map/all_to_all | solution.py:90
  940.9 37.1 %all-to-all-start.2 = ((f32[128,32,3]{1,2,0:T(4,128)}), f32[128,32,3]{1,2,0:T(4,128)S(1)}, u32[]{:S(2)}, u32[]{:S(2)}) async-start(f32[128,32,3]{1,2,0:T(4,128)} %copy.103), calls=%async_computation.2 | async-start | bytes 524288 | tf_op jit(solution)/shard_map/all_to_all | solution.py:90
  (7 other events, 85.8 us)
where the time goes:
time: 1020 us; the launch traced here: 1000 us
  other arithmetic  549 us (54%)
  local copies, waits for them, and re-layouts  358 us (35%)
  starting transfers between devices  75.8 us (7%)
  waiting for transfers between devices  13 us (1%)
    scatter-add x4, other arithmetic, element_terms(): jax.ops.segment_sum(values, target_part, own_nodes + 1)  441 us
    gather x4, local copies, waits for them, and re-layouts, element_terms(): jnp.take(source, conn_part.reshape(-1), axis=1).reshape(COMP, 64, count)  176 us
    select_n x5, other arithmetic, element_terms(): jnp.take(source, conn_part.reshape(-1), axis=1).reshape(COMP, 64, count)  52.6 us
    scatter-add x2, other arithmetic, on_device(): load = jax.ops.segment_sum(moved.reshape(-1, 3), names.reshape(-1), S_DEV)  46 us
    ppermute x8, starting transfers between devices, with_halo(): before = lax.ppermute(last, axis, up)  29.4 us
    reshape x8, local copies, waits for them, and re-layouts, element_terms(): elem_out = elem_out.reshape(COMP, 64 * count)  28.1 us
    select_n x4, local copies, waits for them, and re-layouts, element_terms(): jnp.take(source, conn_part.reshape(-1), axis=1).reshape(COMP, 64, count)  27.5 us
    reshape x8, local copies, waits for them, and re-layouts, on_device(): extended = extended.reshape(COMP, -1)  21.7 us
  transfers between devices with their start and end apart: 19, of which 4 were waited for; matrix products, arithmetic and copies ran while one was open for 49% of the time, Pallas kernels for 0%

commit v1 on v0

v1 whole, which is shorter than its diff:
```python
import functools
import jax
import jax.numpy as jnp
from jax import lax
from jax.experimental import pallas as pl
from jax.experimental.pallas import tpu as pltpu
from jax.sharding import PartitionSpec as P

COMP = 6
ROWS = 32
COLS = 384
ELEMS = 338
IF_CAP = 2048
CAP = 32
ITERS = 2
SWEEPS = 2
LANES = 512
W = 8
F32 = jnp.float32
BF16 = jnp.bfloat16
MESH = pl.DeviceIdType.MESH
NT = (((1,), (1,)), ((), ()))


def iota(shape, dim):
    return lax.broadcasted_iota(jnp.int32, shape, dim)


def onehot(mask):
    return jnp.where(mask, 1.0, 0.0).astype(BF16)


def mm(a, b):
    return jnp.dot(a, b, preferred_element_type=F32)


def mm_nt(a, b):
    return lax.dot_general(a, b, NT, preferred_element_type=F32)


def pieces(x, n):
    out = []
    for k in range(n):
        p = x.astype(BF16)
        out.append(p)
        if k + 1 < n:
            x = x - p.astype(F32)
    return out


def total(terms):
    terms = list(terms)
    while len(terms) > 1:
        terms = [
            terms[i] + terms[i + 1] if i + 1 < len(terms) else terms[i]
            for i in range(0, len(terms), 2)
        ]
    return terms[0]


def pick(x, sel, n=3):
    return total([mm(p, sel) for p in pieces(x, n)])


def pick_rows(sel, x, n=3):
    return total([mm(sel, p) for p in pieces(x, n)])


def ext_col(lane):
    j = lane >> 4
    return jnp.where(j == 25, 374, 15 * j) + (lane & 15)


def kernel(
    G,
    S,
    adj_ref,
    obj_ref,
    diag_ref,
    conn_ref,
    scale_ref,
    em_ref,
    tm_ref,
    node_ref,
    dest_ref,
    target_ref,
    count_ref,
    out_ref,
    load_ref,
    state,
    asm,
    scale_x,
    oi,
    inv,
    wmat,
    conn_raw,
    conn_sem,
    conn_pad,
    scale_pad,
    colhot,
    desthot,
    slot_s,
    rowsend,
    rowrecv,
    colsend,
    colrecv,
    abuf,
    r1,
    r1t,
    r3,
    halo_send,
    halo_recv,
    a1_send,
    a1_recv,
    a2_send,
    a2_recv,
):
    X = S // W
    D = G * S
    g = lax.axis_index("group")
    s = lax.axis_index("sub")
    x = s // W
    w = s % W

    def at(dg, ds):
        return (lax.rem(g + dg + G, G), lax.rem(s + ds + S, S))

    def at_gx(dg, dx):
        return (lax.rem(g + dg, G), lax.rem(x + dx, X) * W + w)

    def at_w(dw):
        return (g, x * W + lax.rem(w + dw, W))

    halo_partners = [(-1, 0), (1, 0)] + [(dg, ds) for ds in (-1, 1) for dg in (-1, 0, 1)]
    gx_partners = [(dg, dx) for dg in range(G) for dx in range(X)][1:]
    barrier = pltpu.get_barrier_semaphore()
    targets = [at(*p) for p in halo_partners]
    targets += [at_gx(*p) for p in gx_partners] + [at_w(dw) for dw in range(1, W)]
    for t in targets:
        pl.semaphore_signal(barrier, inc=1, device_id=t, device_id_type=MESH)

    conn_copy = pltpu.make_async_copy(conn_ref.at[0:8], conn_raw, conn_sem)
    conn_copy.start()
    lane8 = iota((8, 128), 1)

    def halo_copies(t):
        copies = []

        def add(src, dst, dev):
            n = len(copies)
            copies.append(
                pltpu.make_async_remote_copy(
                    src_ref=src,
                    dst_ref=dst,
                    send_sem=halo_send.at[t, n],
                    recv_sem=halo_recv.at[t, n],
                    device_id=dev,
                    device_id_type=MESH,
                )
            )

        add(rowsend.at[t, 0], rowrecv.at[t, 1], at(-1, 0))
        add(rowsend.at[t, 1], rowrecv.at[t, 0], at(1, 0))
        for side, ds in ((0, -1), (1, 1)):
            for dg in (-1, 0, 1):
                add(colsend.at[t, side], colrecv.at[t, 1 - side, 1 - dg], at(dg, ds))
        return copies

    def halo_start(t):
        rowsend[t, 0] = state[1]
        rowsend[t, 1, 0] = state[10, 2]
        rowsend[t, 1, 1] = state[11, 0]
        rowsend[t, 1, 2] = state[11, 1]
        left, right = [], []
        for p in range(ROWS):
            i, a = divmod(p + 3, 3)
            v = jnp.where((lane8 >= 3) & (lane8 < 6), state[i, a, :, 0:128], 0.0)
            left.append(pltpu.roll(v, (3 * p - 3) % 128, 1))
            v = jnp.where((lane8 >= 26) & (lane8 < 29), state[i, a, :, 384:512], 0.0)
            right.append(pltpu.roll(v, (3 * p - 26) % 128, 1))
        colsend[t, 0] = total(left)
        colsend[t, 1] = total(right)
        copies = halo_copies(t)
        if t == 0:
            pl.semaphore_wait(barrier, len(targets))
        for c in copies:
            c.start()
        return copies

    def halo_finish(t, copies):
        for c in copies:
            c.wait_recv()
        state[0] = rowrecv[t, 0]
        state[11, 2] = rowrecv[t, 1, 0]
        state[12, 0] = rowrecv[t, 1, 1]
        state[12, 1] = rowrecv[t, 1, 2]
        bufs = [[colrecv[t, side, k] for k in range(3)] for side in range(2)]
        for r in range(ROWS + 6):
            i, a = divmod(r, 3)
            k, p = (0, 29 + r) if r < 3 else ((1, r - 3) if r < 35 else (2, r - 35))
            v = pltpu.roll(bufs[0][k], (-3 * p) % 128, 1)
            state[i, a, :, 0:128] = state[i, a, :, 0:128] + jnp.where(lane8 < 3, v, 0.0)
            v = pltpu.roll(bufs[1][k], (29 - 3 * p) % 128, 1)
            state[i, a, :, 384:512] = state[i, a, :, 384:512] + jnp.where(
                (lane8 >= 29) & (lane8 < 32), v, 0.0
            )

    lane = iota((COLS, LANES), 1)
    sel = onehot((ext_col(lane) == iota((COLS, LANES), 0) + 3) & (lane < 416))
    m = iota((ROWS * 8, COMP * ROWS), 0)
    perm = onehot(((m & 7) * ROWS + (m >> 3) == iota((ROWS * 8, COMP * ROWS), 1)) & ((m & 7) < COMP))

    def set_own(ref, value):
        v = value.reshape(ROWS, 8, LANES)
        ref[1:11] = v[:30].reshape(10, 3, 8, LANES)
        ref[11, 0:2] = v[30:]

    state[...] = jnp.zeros_like(state)
    first = pick_rows(perm, adj_ref[...].reshape(COMP * ROWS, COLS))
    set_own(state, pick(first, sel))
    copies = halo_start(0)

    inverse = 1.0 / diag_ref[...]
    scaled_obj = obj_ref[...] * inverse[None]
    oi[...] = jnp.zeros_like(oi)
    inv[...] = jnp.zeros_like(inv)
    set_own(oi, pick(pick_rows(perm, scaled_obj.reshape(COMP * ROWS, COLS)), sel))
    rows_8 = jnp.broadcast_to(inverse[:, None, :], (ROWS, 8, COLS)).reshape(ROWS * 8, COLS)
    set_own(inv, pick(rows_8, sel))

    conn_pad[...] = jnp.full_like(conn_pad, -1)
    conn_copy.wait()
    conn_pad[:, 0:ELEMS] = conn_raw[...]
    scale_pad[...] = jnp.zeros_like(scale_pad)
    scale_pad[:, 0:ELEMS] = scale_ref[...]
    node0 = conn_pad[0:1]
    row0 = lax.div(node0, jnp.int32(390))
    col0 = node0 - row0 * 390
    elem_i = jnp.where(node0 >= 0, lax.div(row0 + 2, jnp.int32(3)), -1)
    elem_j = jnp.where(node0 >= 0, lax.div(col0 + 14, jnp.int32(15)), -1)
    row_hot = onehot(elem_i == (iota((112, 384), 0) >> 3))
    i_of = iota((112, LANES), 0) >> 3
    start_row = jnp.minimum(3 * i_of, ROWS + 2)
    lane = iota((112, LANES), 1)
    off_left = (s == 0) & (lane < 3)
    off_right = (s == S - 1) & (lane >= 413)
    j_mask = elem_j[:, None, :] == iota((32, 16, 384), 0)
    for a in range(4):
        sc = scale_pad[16 * a : 16 * a + 16]
        out = []
        for p in pieces(sc, 3):
            p = jnp.where(j_mask, p.astype(F32)[None], 0.0).reshape(LANES, 384)
            out.append(mm_nt(row_hot, p.astype(BF16)))
        r = start_row + a
        off = ((g == 0) & (r < 3)) | ((g == G - 1) & (r >= ROWS + 3)) | off_left | off_right
        scale_x[a] = jnp.where(off, 0.0, total(out)).reshape(14, 8, LANES)

    r = iota((LANES, 64), 0)
    e_hot = onehot((r >> 7) * 16 + (r & 15) == iota((LANES, 64), 1))
    left = mm(e_hot, em_ref[...]).astype(BF16)
    rr, cc = iota((LANES, LANES), 0), iota((LANES, LANES), 1)
    wide = mm_nt(left, e_hot)
    wmat[...] = jnp.where(((rr >> 4) & 7) == ((cc >> 4) & 7), wide, 0.0).astype(BF16)

    def sweep():
        for q in range(4):
            cols = slice(128 * q, 128 * q + 128)
            parts = []
            for a in range(4):
                main = state[0:12, a, :, cols] if a < 3 else state[1:13, 0, :, cols]
                i, b = [(11, 1), (11, 2), (12, 0), (12, 1)][a]
                last = state[i, b, :, cols][None]
                v = jnp.concatenate([main, last, jnp.zeros_like(last)], axis=0)
                v = v * scale_x[a, :, :, cols]
                parts.append(v.reshape(112, 128).astype(BF16))
            o = mm(jnp.concatenate(parts, axis=1), wmat[...])
            o = [o[:, 128 * a : 128 * a + 128].reshape(14, 8, 128) for a in range(4)]
            asm[:, 0, :, cols] = o[0][1:12] + o[3][0:11]
            asm[0:10, 1, :, cols] = o[1][1:11]
            asm[10, 1, :, cols] = o[1][11] + o[0][12]
            asm[:, 2, :, cols] = o[2][1:12]
        lane = iota((24, 128), 1)
        low = lane & 15
        for i in range(11):
            tiles = [asm[i, :, :, 128 * q : 128 * q + 128].reshape(24, 128) for q in range(4)]
            up = [pltpu.roll(v, 1, 1) for v in tiles]
            down = [pltpu.roll(v, 127, 1) for v in tiles]
            for q in range(4):
                before = up[q] if q == 0 else jnp.where(lane == 0, up[q - 1], up[q])
                after = down[q] if q == 3 else jnp.where(lane == 127, down[q + 1], down[q])
                if q < 3:
                    more = jnp.where(low == 0, before, jnp.where(low == 15, after, 0.0))
                    if q == 0:
                        more = jnp.where(lane == 0, 0.0, more)
                else:
                    more = jnp.where(lane == 0, before, 0.0)
                    more = jnp.where(
                        (lane == 14) | (lane == 15), pltpu.roll(tiles[3], 126, 1), more
                    )
                    more = jnp.where(
                        (lane == 16) | (lane == 17), pltpu.roll(tiles[3], 2, 1), more
                    )
                cols = slice(128 * q, 128 * q + 128)
                whole = (tiles[q] + more).reshape(3, 8, 128)
                state[i + 1, :, :, cols] = oi[i + 1, :, :, cols] - whole * inv[i + 1, :, :, cols]

    CH = 512
    node = node_ref[...]
    node_row = lax.div(node, jnp.int32(COLS))
    e_col = node - node_row * COLS + 3
    e_lane = jnp.where(e_col < 375, e_col + lax.div(e_col, jnp.int32(15)), e_col + 26)

    def setup_rows():
        live = iota((1, IF_CAP), 1) < count_ref[0]
        dest = jnp.where(live, dest_ref[...], -1)
        tri = onehot(iota((256, 256), 0) < iota((256, 256), 1))
        carry = jnp.zeros((D, 1), F32)
        for b in range(IF_CAP // 256):
            cols = slice(256 * b, 256 * b + 256)
            hot = jnp.where(dest[:, cols] == iota((D, 256), 0), 1.0, 0.0)
            desthot[:, cols] = hot.astype(BF16)
            before = mm(hot.astype(BF16), tri) + carry
            slot_s[:, cols] = jnp.sum(before * hot, axis=0, keepdims=True)
            carry = carry + jnp.sum(hot, axis=1, keepdims=True)
        for b in range(IF_CAP // CH):
            cols = slice(CH * b, CH * b + CH)
            colhot[:, cols] = onehot(e_lane[:, cols] == iota((LANES, CH), 0))

    def gather(t):
        lane = iota((1, 256), 1)
        trac = []
        for k in range(3):
            row = jnp.zeros((1, 256), F32)
            for c in range(COMP):
                row = jnp.where((lane & 7) == c, tm_ref[k, c], row)
            trac.append(jnp.where((iota((32, 256), 1) >> 3) == iota((32, 256), 0), row, 0.0))
        trac = jnp.concatenate(trac, axis=0)
        own = jnp.concatenate(
            [state[1:11].reshape(240, LANES), state[11, 0:2].reshape(16, LANES)], axis=0
        )
        field = jnp.dot(trac, own, precision=lax.Precision.HIGHEST, preferred_element_type=F32)
        field = jnp.concatenate(pieces(field, 2), axis=0)
        acc = jnp.zeros((D, 128), F32)
        for b in range(IF_CAP // CH):
            cols = slice(CH * b, CH * b + CH)
            v = mm(field, colhot[:, cols])
            v = (v[:96] + v[96:]).reshape(3, 32, CH)
            v = jnp.where(node_row[:, cols][None] == iota((3, 32, CH), 1), v, 0.0)
            v = jnp.sum(v, axis=1, keepdims=True)
            v = jnp.concatenate([v, target_ref[:, cols].astype(F32)[None]], axis=0)
            slots = slot_s[:, cols].astype(jnp.int32)[None] == iota((4, CAP, CH), 1)
            v = jnp.where(slots, v, 0.0).reshape(4 * CAP, CH)
            for p in pieces(v, 2):
                acc = acc + mm_nt(desthot[:, cols], p)
        abuf[t] = acc.reshape(D // 8, 8, 128)

    def a2a_1(t):
        copies = []
        for o, (dg, dx) in enumerate(gx_partners):
            to_g, to_s = at_gx(dg, dx)
            copies.append(
                pltpu.make_async_remote_copy(
                    src_ref=abuf.at[t, to_g * X + to_s // W],
                    dst_ref=r1.at[t, pl.ds(8 * (o + 1), 8)],
                    send_sem=a1_send.at[t, o],
                    recv_sem=a1_recv.at[t, o],
                    device_id=(to_g, to_s),
                    device_id_type=MESH,
                )
            )
            copies[-1].start()
        r1[t, 0:8] = abuf[t, g * X + x]
        return copies

    def a2a_2(t, first):
        for c in first:
            c.wait_recv()
        for d in range(W):
            r1t[t, d] = r1[t, pl.ds(d, D // W, stride=W), :]
        copies = []
        for dw in range(1, W):
            to = at_w(dw)
            copies.append(
                pltpu.make_async_remote_copy(
                    src_ref=r1t.at[t, lax.rem(w + dw, W)],
                    dst_ref=r3.at[t, dw],
                    send_sem=a2_send.at[t, dw - 1],
                    recv_sem=a2_recv.at[t, dw - 1],
                    device_id=to,
                    device_id_type=MESH,
                )
            )
            copies[-1].start()
        r3[t, 0] = r1t[t, w]
        return copies

    def place(t, second):
        for c in second:
            c.wait_recv()
        got = r3[t].reshape(D, 128).T
        name = got[96:128]
        high = jnp.floor(name * (1.0 / 128.0))
        low = name - 128.0 * high
        acc = jnp.zeros((96, 128), F32)
        for q in range(CAP // 4):
            left, right = [], []
            for z in range(4 * q, 4 * q + 4):
                right.append(onehot(low[z : z + 1] == iota((128, D), 0).astype(F32)))
                hit = high[z : z + 1] == iota((16, D), 0).astype(F32)
                v = jnp.concatenate(
                    [jnp.where(hit, got[32 * k + z : 32 * k + z + 1], 0.0) for k in range(3)], axis=0
                )
                left.append(jnp.concatenate(pieces(v, 2), axis=0))
            acc = acc + mm_nt(jnp.concatenate(left, axis=1), jnp.concatenate(right, axis=1))
        acc = acc[:48] + acc[48:]
        for k in range(3):
            for h in range(16):
                load_ref[t, k : k + 1, 128 * h : 128 * h + 128] = acc[16 * k + h : 16 * k + h + 1]

    def write_adjoint():
        own = jnp.concatenate(
            [state[1:11].reshape(240, LANES), state[11, 0:2].reshape(16, LANES)], axis=0
        )
        lane = iota((LANES, COLS), 0)
        j, b = lane >> 4, lane & 15
        keep = ((j < 25) & (b < 15)) | ((j == 25) & (b > 0))
        back = onehot(keep & (ext_col(lane) == iota((LANES, COLS), 1) + 3))
        n = iota((COMP * ROWS, ROWS * 8), 1)
        unperm = onehot((n & 7) * ROWS + (n >> 3) == iota((COMP * ROWS, ROWS * 8), 0))
        out_ref[...] = pick_rows(unperm, pick(own, back)).reshape(COMP, ROWS, COLS)

    sent = list(copies)
    halo_finish(0, copies)
    sweep()
    copies = halo_start(1)
    sent += copies
    setup_rows()
    halo_finish(1, copies)
    sweep()
    copies = halo_start(2)
    sent += copies
    gather(0)
    first = a2a_1(0)
    sent += first
    halo_finish(2, copies)
    sweep()
    copies = halo_start(3)
    sent += copies
    second = a2a_2(0, first)
    sent += second
    halo_finish(3, copies)
    sweep()
    gather(1)
    first = a2a_1(1)
    sent += first
    place(0, second)
    second = a2a_2(1, first)
    sent += second
    write_adjoint()
    place(1, second)
    for c in sent:
        c.wait_send()


def on_device(
    G,
    S,
    adjoint_start,
    objective_grad,
    diagonal,
    connect,
    element_scale,
    element_matrix,
    traction_map,
    iface_node,
    iface_dest,
    iface_target,
    iface_count,
):
    vmem = pl.BlockSpec(memory_space=pltpu.VMEM)
    smem = pl.BlockSpec(memory_space=pltpu.SMEM)
    D = G * S
    XG = D // W
    dma = pltpu.SemaphoreType.DMA
    scratch = [
        pltpu.VMEM((13, 3, 8, LANES), F32),
        pltpu.VMEM((11, 3, 8, LANES), F32),
        pltpu.VMEM((4, 14, 8, LANES), F32),
        pltpu.VMEM((12, 3, 8, LANES), F32),
        pltpu.VMEM((12, 3, 8, LANES), F32),
        pltpu.VMEM((LANES, LANES), BF16),
        pltpu.VMEM((8, ELEMS), jnp.int32),
        dma,
        pltpu.VMEM((8, 384), jnp.int32),
        pltpu.VMEM((64, 384), F32),
        pltpu.VMEM((LANES, IF_CAP), BF16),
        pltpu.VMEM((D, IF_CAP), BF16),
        pltpu.VMEM((1, IF_CAP), F32),
        pltpu.VMEM((4, 2, 3, 8, LANES), F32),
        pltpu.VMEM((4, 2, 3, 8, LANES), F32),
        pltpu.VMEM((4, 2, 8, 128), F32),
        pltpu.VMEM((4, 2, 3, 8, 128), F32),
        pltpu.VMEM((ITERS, XG, 8, 128), F32),
        pltpu.VMEM((ITERS, D, 128), F32),
        pltpu.VMEM((ITERS, W, XG, 128), F32),
        pltpu.VMEM((ITERS, W, XG, 128), F32),
        dma((4, 8)),
        dma((4, 8)),
        dma((ITERS, XG - 1)),
        dma((ITERS, XG - 1)),
        dma((ITERS, W - 1)),
        dma((ITERS, W - 1)),
    ]
    call = pl.pallas_call(
        functools.partial(kernel, G, S),
        out_shape=(
            jax.ShapeDtypeStruct((COMP, ROWS, COLS), F32),
            jax.ShapeDtypeStruct((ITERS, 3, IF_CAP), F32),
        ),
        in_specs=[vmem, vmem, vmem, pl.BlockSpec(memory_space=pl.ANY), vmem, vmem, smem]
        + [vmem] * 3
        + [smem],
        out_specs=(vmem, vmem),
        scratch_shapes=scratch,
        compiler_params=pltpu.CompilerParams(
            collective_id=0, has_side_effects=True, vmem_limit_bytes=40 * 1024 * 1024
        ),
    )
    return call(
        adjoint_start,
        objective_grad,
        diagonal,
        connect,
        element_scale,
        element_matrix,
        traction_map,
        iface_node.reshape(1, IF_CAP),
        iface_dest.reshape(1, IF_CAP),
        iface_target.reshape(1, IF_CAP),
        iface_count,
    )


def solution(mesh):
    both = ("group", "sub")
    placed = (
        P(None, "group", "sub"),
        P(None, "group", "sub"),
        P("group", "sub"),
        P(None, both),
        P(None, both),
        P(),
        P(),
        P(both),
        P(both, None),
        P(both),
        P(both),
    )
    return jax.shard_map(
        functools.partial(on_device, mesh.shape["group"], mesh.shape["sub"]),
        mesh=mesh,
        in_specs=placed,
        out_specs=(P(None, "group", "sub"), P(None, None, both)),
        check_vma=False,
    )
```

time: 1020 us -> 54.2 us (0.05); the launches traced: 1000 us -> 53.7 us
  other arithmetic: 549 us -> 0 us
  local copies, waits for them, and re-layouts: 358 us -> 9.36 us
  starting transfers between devices: 75.8 us -> 0 us
  Pallas kernels: 0 us -> 43 us
  waiting for transfers between devices: 13 us -> 0 us
    scatter-add x6 -> x0, other arithmetic: 487 us -> none  [the longest x4 441 us: element_terms(): jax.ops.segment_sum(values, target_part, own_nodes + 1)]
    gather x6 -> x0, local copies, waits for them, and re-layouts: 192 us -> none  [the longest x4 176 us: element_terms(): jnp.take(source, conn_part.reshape(-1), axis=1).reshape(COMP, 64, count)]
    reshape x29 -> x0, local copies, waits for them, and re-layouts: 80.1 us -> none  [the longest x8 28.1 us: element_terms(): elem_out = elem_out.reshape(COMP, 64 * count)]
    select_n x7 -> x0, other arithmetic: 53.6 us -> none  [the longest x5 52.6 us: element_terms(): jnp.take(source, conn_part.reshape(-1), axis=1).reshape(COMP, 64, count)]
    pallas_call x0 -> x1, Pallas kernels: none -> 43 us  [on_device(): call(adjoint_start, objective_grad, diagonal, connect, element_scale, ele...]
    ppermute x16 -> x0, starting transfers between devices: 42.8 us -> none  [the longest x8 29.4 us: with_halo(): before = lax.ppermute(last, axis, up)]
    all_to_all x3 -> x0, starting transfers between devices: 33 us -> none  [the longest x2 21 us: on_device(): lax.all_to_all(buffer.reshape(devices, cap, 3), ('group', 'sub'), split_a...]
    select_n x6 -> x0, local copies, waits for them, and re-layouts: 30.2 us -> none  [the longest x4 27.5 us: element_terms(): jnp.take(source, conn_part.reshape(-1), axis=1).reshape(COMP, 64, count)]
  transfers between devices with their start and end apart: 19 -> 0, of which waited for: 4 -> 0; matrix products, arithmetic and copies ran while one was open for 49% -> 0% of each run, Pallas kernels for 0% -> 0%
where the time goes in v1:
time: 54.2 us; the launch traced here: 53.7 us
  Pallas kernels  43 us (79%)
  local copies, waits for them, and re-layouts  9.36 us (17%)
  between operations  1.31 us (2%)
    pallas_call x1, Pallas kernels, on_device(): call(adjoint_start, objective_grad, diagonal, connect, element_scale, ele...  43 us
    unnamed x21, local copies, waits for them, and re-layouts  8.7 us

profile of v1, /device:TPU:1, one launch (start us, length us, event | category | flops | bytes accessed | tf_op | source)
XLA Modules:
  0.0 53.7 jit_solution(11979654609782614241)
XLA Ops:
  1.3 0.0 copy-start.9
  1.3 0.7 %copy-done.9 = f32[3,6]{1,0:T(4,128)S(1)} copy-done((f32[3,6]{1,0:T(4,128)S(1)}, f32[3,6]{1,0:T(4,128)}, u32[]{:S(2)}) %copy-start.9) | copy-done | bytes 96
  2.0 0.0 copy-start
  2.0 1.0 %copy-done = f32[6,32,384]{2,1,0:T(8,128)S(1)} copy-done((f32[6,32,384]{2,1,0:T(8,128)S(1)}, f32[6,32,384]{2,1,0:T(8,128)}, u32[]{:S(2)}) %copy-start) | copy-done | bytes 294936
  2.9 0.0 copy-start.1
  2.9 1.0 %copy-done.1 = f32[6,32,384]{2,1,0:T(8,128)S(1)} copy-done((f32[6,32,384]{2,1,0:T(8,128)S(1)}, f32[6,32,384]{2,1,0:T(8,128)}, u32[]{:S(2)}) %copy-start.1) | copy-done | bytes 294936
  3.9 0.0 copy-start.2
  3.9 0.9 %copy-done.2 = s32[64,338]{1,0:T(8,128)S(1)} copy-done((s32[64,338]{1,0:T(8,128)S(1)}, s32[64,338]{1,0:T(8,128)}, u32[]{:S(2)}) %copy-start.2) | copy-done | bytes 86552
  4.8 0.0 copy-start.3
  4.8 0.9 %copy-done.3 = f32[64,338]{1,0:T(8,128)S(1)} copy-done((f32[64,338]{1,0:T(8,128)S(1)}, f32[64,338]{1,0:T(8,128)}, u32[]{:S(2)}) %copy-start.3) | copy-done | bytes 86552
  5.7 0.0 copy-start.4
  5.7 0.8 %copy-done.4 = f32[32,384]{1,0:T(8,128)S(1)} copy-done((f32[32,384]{1,0:T(8,128)S(1)}, f32[32,384]{1,0:T(8,128)}, u32[]{:S(2)}) %copy-start.4) | copy-done | bytes 49176
  6.5 0.0 copy-start.5
  6.5 0.7 %copy-done.5 = bf16[64,64]{1,0:T(8,128)(2,1)S(1)} copy-done((bf16[64,64]{1,0:T(8,128)(2,1)S(1)}, bf16[64,64]{1,0:T(8,128)(2,1)}, u32[]{:S(2)}) %copy-start.5) | copy-done | bytes 8216
  7.2 0.0 copy-start.6
  7.2 0.7 %copy-done.6 = s32[2048]{0:T(1024)S(1)} copy-done((s32[2048]{0:T(1024)S(1)}, s32[2048]{0:T(1024)}, u32[]{:S(2)}) %copy-start.6) | copy-done | bytes 8216
  7.9 0.0 copy-start.7
  7.9 0.7 %copy-done.7 = s32[2048,1]{0,1:T(1,128)S(1)} copy-done((s32[2048,1]{0,1:T(1,128)S(1)}, s32[2048,1]{0,1:T(1,128)}, u32[]{:S(2)}) %copy-start.7) | copy-done | bytes 8216
  8.6 0.0 copy-start.8
  8.6 0.7 %copy-done.8 = s32[2048]{0:T(1024)S(1)} copy-done((s32[2048]{0:T(1024)S(1)}, s32[2048]{0:T(1024)}, u32[]{:S(2)}) %copy-start.8) | copy-done | bytes 8216
  9.3 43.0 %shard_map.122 = (f32[6,32,384]{2,1,0:T(8,128)S(1)}, f32[2,3,2048]{2,1,0:T(4,128)S(1)}) custom-call(f32[6,32,384]{2,1,0:T(8,128)S(1)} %copy-done, f32[6,32,384]{2,1,0:T(8,128)S(1)} %copy-done.1, f32[32,384]{1,0:T(8,128)S(1)} %copy-done.4, s32[64,338]{1,0:T(8,128)S(1)} %copy-done.2, f32[64,338]{1,0:T(8,128)S(1)} %copy-done.3, bf16[64,64]{1,0:T(8,128)(2,1)S(1)} %copy-done.5, ...), custom_call_target="tpu_custom_call" | custom-call | tf_op jit(solution)/shard_map/pallas_call | solution.py:529
  52.3 0.7 %copy.13 = f32[2,3,2048]{2,0,1:T(2,128)} copy(f32[2,3,2048]{2,1,0:T(4,128)S(1)} %get-tuple-element.3) | data formatting | bytes 98304 | tf_op jit(solution)/shard_map/pallas_call | solution.py:529
  52.9 0.7 %copy.16 = f32[6,32,384]{2,1,0:T(8,128)} copy(f32[6,32,384]{2,1,0:T(8,128)S(1)} %get-tuple-element.6) | data formatting | bytes 589824
Async XLA Ops:
  1.3 0.7 %copy-start.9 = (f32[3,6]{1,0:T(4,128)S(1)}, f32[3,6]{1,0:T(4,128)}, u32[]{:S(2)}) copy-start(f32[3,6]{1,0:T(4,128)} %tm_ref.1) | copy-start | bytes 220
  2.0 1.0 %copy-start = (f32[6,32,384]{2,1,0:T(8,128)S(1)}, f32[6,32,384]{2,1,0:T(8,128)}, u32[]{:S(2)}) copy-start(f32[6,32,384]{2,1,0:T(8,128)} %adj_ref.1) | copy-start | bytes 884740
  2.9 1.0 %copy-start.1 = (f32[6,32,384]{2,1,0:T(8,128)S(1)}, f32[6,32,384]{2,1,0:T(8,128)}, u32[]{:S(2)}) copy-start(f32[6,32,384]{2,1,0:T(8,128)} %obj_ref.1) | copy-start | bytes 884740
  3.9 0.9 %copy-start.2 = (s32[64,338]{1,0:T(8,128)S(1)}, s32[64,338]{1,0:T(8,128)}, u32[]{:S(2)}) copy-start(s32[64,338]{1,0:T(8,128)} %conn_ref.1) | copy-start | bytes 259588
  4.8 0.9 %copy-start.3 = (f32[64,338]{1,0:T(8,128)S(1)}, f32[64,338]{1,0:T(8,128)}, u32[]{:S(2)}) copy-start(f32[64,338]{1,0:T(8,128)} %scale_ref.1) | copy-start | bytes 259588
  5.7 0.8 %copy-start.4 = (f32[32,384]{1,0:T(8,128)S(1)}, f32[32,384]{1,0:T(8,128)}, u32[]{:S(2)}) copy-start(f32[32,384]{1,0:T(8,128)} %diag_ref.1) | copy-start | bytes 147460
  6.5 0.7 %copy-start.5 = (bf16[64,64]{1,0:T(8,128)(2,1)S(1)}, bf16[64,64]{1,0:T(8,128)(2,1)}, u32[]{:S(2)}) copy-start(bf16[64,64]{1,0:T(8,128)(2,1)} %em_ref.1) | copy-start | bytes 24580
  7.2 0.7 %copy-start.6 = (s32[2048]{0:T(1024)S(1)}, s32[2048]{0:T(1024)}, u32[]{:S(2)}) copy-start(s32[2048]{0:T(1024)} %param.18) | copy-start | bytes 24580
  7.9 0.7 %copy-start.7 = (s32[2048,1]{0,1:T(1,128)S(1)}, s32[2048,1]{0,1:T(1,128)}, u32[]{:S(2)}) copy-start(s32[2048,1]{0,1:T(1,128)} %param.19) | copy-start | bytes 24580
  8.6 0.7 %copy-start.8 = (s32[2048]{0:T(1024)S(1)}, s32[2048]{0:T(1024)}, u32[]{:S(2)}) copy-start(s32[2048]{0:T(1024)} %param.20) | copy-start | bytes 24580

commit v2 on v1

v2 whole, which is shorter than its diff:
```python
import functools
import jax
import jax.numpy as jnp
from jax import lax
from jax.experimental import pallas as pl
from jax.experimental.pallas import tpu as pltpu
from jax.sharding import PartitionSpec as P

COMP = 6
ROWS = 32
COLS = 384
ELEMS = 338
IF_CAP = 2048
CAP = 32
ITERS = 2
SWEEPS = 2
LANES = 512
UP, DOWN = 11, 10
O_UP, O_DOWN = 8, 7
STARTS = (
    [-11, -8, -5, -2, -1] + [min(3 * i, ROWS + 2) - 3 for i in range(13)] + [29, 32, 35, 38]
)
ACTIVE = [(0, 22), (1, 21), (2, 20), (4, 18)]
UPDATED = [(-8, 39), (-5, 36), (-3, 35), (0, 32)]
W = 8
F32 = jnp.float32
BF16 = jnp.bfloat16
MESH = pl.DeviceIdType.MESH
NT = (((1,), (1,)), ((), ()))


def iota(shape, dim):
    return lax.broadcasted_iota(jnp.int32, shape, dim)


def onehot(mask):
    return jnp.where(mask, 1.0, 0.0).astype(BF16)


def mm(a, b):
    return jnp.dot(a, b, preferred_element_type=F32)


def mm_nt(a, b):
    return lax.dot_general(a, b, NT, preferred_element_type=F32)


def pieces(x, n):
    out = []
    for k in range(n):
        p = x.astype(BF16)
        out.append(p)
        if k + 1 < n:
            x = x - p.astype(F32)
    return out


def total(terms):
    terms = list(terms)
    while len(terms) > 1:
        terms = [
            terms[i] + terms[i + 1] if i + 1 < len(terms) else terms[i]
            for i in range(0, len(terms), 2)
        ]
    return terms[0]


def pick(x, sel, n=3):
    return total([mm(p, sel) for p in pieces(x, n)])


def pick_rows(sel, x, n=3):
    return total([mm(sel, p) for p in pieces(x, n)])


def ext_col(lane):
    j = lane >> 4
    return jnp.where(j == 25, 374, 15 * j) + (lane & 15)


def owner(row):
    return 0 if row < 0 else (1 if row < ROWS else 2)


def block_of(e):
    return 0 if e < 5 else (1 if e < 18 else 2)


def kernel(
    G,
    S,
    adj_hbm,
    obj_hbm,
    diag_hbm,
    conn_hbm,
    scale_hbm,
    em_hbm,
    tm_hbm,
    node_hbm,
    dest_hbm,
    target_hbm,
    count_hbm,
    out_ref,
    load_ref,
    adj_ref,
    obj_ref,
    diag_ref,
    conn_ref,
    scale_ref,
    em_ref,
    tm_ref,
    node_ref,
    dest_ref,
    target_ref,
    count_ref,
    in_sem,
    state,
    oi,
    asm,
    scale_own,
    scale_up,
    scale_down,
    wmat,
    conn_pad,
    scale_pad,
    colhot,
    desthot,
    slot_s,
    side_send,
    side_recv,
    sscale_send,
    sscale_recv,
    abuf,
    r1,
    r1t,
    r3,
    halo_send,
    halo_recv,
    a1_send,
    a1_recv,
    a2_send,
    a2_recv,
):
    X = S // W
    D = G * S
    g = lax.axis_index("group")
    s = lax.axis_index("sub")
    x = s // W
    w = s % W

    def at(dg, ds):
        return (lax.rem(g + dg + G, G), lax.rem(s + ds + S, S))

    def at_gx(dg, dx):
        return (lax.rem(g + dg, G), lax.rem(x + dx, X) * W + w)

    def at_w(dw):
        return (g, x * W + lax.rem(w + dw, W))

    loads = [
        pltpu.make_async_copy(src, dst, in_sem.at[n])
        for n, (src, dst) in enumerate(
            [
                (adj_hbm, adj_ref),
                (diag_hbm, diag_ref),
                (obj_hbm, obj_ref),
                (conn_hbm.at[0:8], conn_ref),
                (scale_hbm, scale_ref),
                (em_hbm, em_ref),
                (tm_hbm, tm_ref),
                (node_hbm, node_ref),
                (dest_hbm, dest_ref),
                (target_hbm, target_ref),
                (count_hbm, count_ref),
            ]
        )
    ]
    for c in loads:
        c.start()
    gx_partners = [(dg, dx) for dg in range(G) for dx in range(X)][1:]
    barrier = pltpu.get_barrier_semaphore()
    targets = [at(0, -1), at(0, 1)]
    targets += [at_gx(*p) for p in gx_partners] + [at_w(dw) for dw in range(1, W)]
    for t in targets:
        pl.semaphore_signal(barrier, inc=1, device_id=t, device_id_type=MESH)

    lane = iota((COLS, LANES), 1)
    sel = onehot((ext_col(lane) == iota((COLS, LANES), 0) + 3) & (lane < 416))
    m = iota((ROWS * 8, COMP * ROWS), 0)
    perm = onehot(((m & 7) * ROWS + (m >> 3) == iota((ROWS * 8, COMP * ROWS), 1)) & ((m & 7) < COMP))
    loads[0].wait()
    first = pick_rows(perm, adj_ref[...].reshape(COMP * ROWS, COLS))
    state[UP : UP + ROWS] = pick(first, sel).reshape(ROWS, 8, LANES)

    loads[1].wait()
    loads[2].wait()
    inverse = 1.0 / diag_ref[...]
    scaled_obj = (obj_ref[...] * inverse[None]).reshape(COMP * ROWS, COLS)
    m = iota((ROWS * 8, ROWS), 0)
    perm_inv = onehot(((m & 7) == COMP) & ((m >> 3) == iota((ROWS * 8, ROWS), 1)))
    first = pick_rows(perm, scaled_obj) + pick_rows(perm_inv, inverse)
    oi[O_UP : O_UP + ROWS] = pick(first, sel).reshape(ROWS, 8, LANES)

    loads[3].wait()
    loads[4].wait()
    conn_pad[...] = jnp.full_like(conn_pad, -1)
    conn_pad[:, 0:ELEMS] = conn_ref[...]
    scale_pad[...] = jnp.zeros_like(scale_pad)
    scale_pad[:, 0:ELEMS] = scale_ref[...]
    node0 = conn_pad[0:1]
    row0 = lax.div(node0, jnp.int32(390))
    col0 = node0 - row0 * 390
    elem_i = jnp.where(node0 >= 0, lax.div(row0 + 2, jnp.int32(3)), -1)
    elem_j = jnp.where(node0 >= 0, lax.div(col0 + 14, jnp.int32(15)), -1)
    row_hot = onehot(elem_i == iota((16, 384), 0))
    start_row = jnp.minimum(3 * iota((16, LANES), 0), ROWS + 2)
    lane = iota((16, LANES), 1)
    off_side = ((s == 0) & (lane < 3)) | ((s == S - 1) & (lane >= 413))
    j_mask = elem_j[:, None, :] == iota((32, 16, 384), 0)
    for a in range(4):
        sc = scale_pad[16 * a : 16 * a + 16]
        out = []
        for p in pieces(sc, 3):
            p = jnp.where(j_mask, p.astype(F32)[None], 0.0).reshape(LANES, 384)
            out.append(mm_nt(row_hot, p.astype(BF16)))
        r = start_row + a
        off = ((g == 0) & (r < 3)) | ((g == G - 1) & (r >= ROWS + 3)) | off_side
        scale_own[a] = jnp.where(off, 0.0, total(out))

    def remote(n, src, dst, dev):
        return pltpu.make_async_remote_copy(
            src_ref=src,
            dst_ref=dst,
            send_sem=halo_send.at[n],
            recv_sem=halo_recv.at[n],
            device_id=dev,
            device_id_type=MESH,
        )

    def turn(v, n):
        return pltpu.roll(v, n % 128, v.ndim - 1)

    def pack_right(two, three, start):
        lane = iota(two.shape, two.ndim - 1)
        return jnp.where(lane < start + 16, turn(two, start - 112), turn(three, start + 16))

    for p in range(0, ROWS, 8):
        st = [state[UP + p : UP + p + 8, :, 128 * q : 128 * q + 128] for q in (0, 2, 3)]
        ob = [oi[O_UP + p : O_UP + p + 8, :, 128 * q : 128 * q + 128] for q in (0, 2, 3)]
        lane = iota((8, 8, 128), 2)
        side_send[0, p : p + 8] = jnp.where(lane < 80, turn(st[0], 32), turn(ob[0], 80))
        side_send[1, p : p + 8] = jnp.where(
            lane < 80, pack_right(ob[1], ob[2], 32), pack_right(st[1], st[2], 80)
        )
    for a in range(4):
        sscale_send[0, a] = turn(scale_own[a, :, 0:128], 32)
        sscale_send[1, a] = pack_right(scale_own[a, :, 256:384], scale_own[a, :, 384:512], 80)

    def row_copies(n, cols):
        up, down = at(-1, 0), at(1, 0)
        return [
            remote(n, state.at[UP + ROWS - UP : UP + ROWS, :, cols], state.at[0:UP, :, cols], down),
            remote(
                n + 1,
                state.at[UP : UP + DOWN, :, cols],
                state.at[UP + ROWS : UP + ROWS + DOWN, :, cols],
                up,
            ),
            remote(n + 2, oi.at[ROWS : O_UP + ROWS, :, cols], oi.at[0:O_UP, :, cols], down),
            remote(
                n + 3,
                oi.at[O_UP : O_UP + O_DOWN, :, cols],
                oi.at[O_UP + ROWS : O_UP + ROWS + O_DOWN, :, cols],
                up,
            ),
            remote(n + 4, scale_own.at[:, 8:16, cols], scale_up.at[:, :, cols], down),
            remote(n + 5, scale_own.at[:, 0:8, cols], scale_down.at[:, :, cols], up),
        ]

    pl.semaphore_wait(barrier, len(targets))
    side_copies = [
        remote(0, side_send.at[0], side_recv.at[0], at(0, -1)),
        remote(1, side_send.at[1], side_recv.at[1], at(0, 1)),
        remote(2, sscale_send.at[0], sscale_recv.at[0], at(0, -1)),
        remote(3, sscale_send.at[1], sscale_recv.at[1], at(0, 1)),
    ]
    for c in side_copies:
        c.start()
    row_early = row_copies(4, slice(0, 384))
    for c in row_early:
        c.start()

    loads[5].wait()
    r = iota((LANES, 64), 0)
    e_hot = onehot((r >> 7) * 16 + (r & 15) == iota((LANES, 64), 1))
    left = mm(e_hot, em_ref[...]).astype(BF16)
    rr, cc = iota((LANES, LANES), 0), iota((LANES, LANES), 1)
    wide = mm_nt(left, e_hot)
    wmat[...] = jnp.where(((rr >> 4) & 7) == ((cc >> 4) & 7), wide, 0.0).astype(BF16)

    def sides_finish():
        for c in side_copies:
            c.wait_recv()
        for p in range(0, ROWS, 8):
            lane = iota((8, 8, 128), 2)
            right, left = side_recv[0, p : p + 8], side_recv[1, p : p + 8]
            own = state[UP + p : UP + p + 8, :, 384:512]
            state[UP + p : UP + p + 8, :, 384:512] = jnp.where(
                lane < 32, own, jnp.where(lane < 80, right, left)
            )
            own = oi[O_UP + p : O_UP + p + 8, :, 384:512]
            both = jnp.where(lane < 80, left, right)
            oi[O_UP + p : O_UP + p + 8, :, 384:512] = jnp.where(
                lane < 32, own, jnp.where(lane < 80, turn(both, -48), turn(both, 48))
            )
        lane = iota((16, 128), 1)
        for a in range(4):
            scale_own[a, :, 384:512] = jnp.where(
                lane < 32,
                scale_own[a, :, 384:512],
                jnp.where(lane < 80, sscale_recv[0, a], sscale_recv[1, a]),
            )

    def fill(first, three):
        lane = iota(first.shape, first.ndim - 1)
        ahead = turn(three, 6)
        first_new = jnp.where(lane < 3, ahead, first)
        three_new = jnp.where((lane >= 32) & (lane < 35), ahead, three)
        three_new = jnp.where((lane >= 29) & (lane < 32), turn(three, -6), three_new)
        three_new = jnp.where(lane >= 125, turn(first, -6), three_new)
        return first_new, three_new

    def fill_rows(lo, hi):
        lo, hi = UP + lo, UP + hi
        state[lo:hi, :, 0:128], state[lo:hi, :, 384:512] = fill(
            state[lo:hi, :, 0:128], state[lo:hi, :, 384:512]
        )

    def scale_row(a, e, cols):
        if e < 5:
            v = scale_up[a, e : e + 1, cols]
        elif e < 18:
            v = scale_own[a, e - 5 : e - 4, cols]
        else:
            v = scale_down[a, e - 18 : e - 17, cols]
        return jnp.broadcast_to(v, (8, 128))

    def sweep(t):
        lo, hi = ACTIVE[t]
        rows = range(*UPDATED[t])
        count = hi - lo
        for q in range(4):
            cols = slice(128 * q, 128 * q + 128)
            parts = []
            for a in range(4):
                v = [
                    state[UP + STARTS[e] + a, :, cols] * scale_row(a, e, cols)
                    for e in range(lo, hi)
                ]
                parts.append(jnp.concatenate(v, axis=0).astype(BF16))
            o = mm(jnp.concatenate(parts, axis=1), wmat[...])
            for row in rows:
                terms = [
                    o[8 * (e - lo) : 8 * (e - lo) + 8, 128 * a : 128 * a + 128]
                    for e in range(lo, hi)
                    for a in range(4)
                    if STARTS[e] + a == row and block_of(e) == owner(row)
                ]
                asm[O_UP + row, :, cols] = total(terms)
        step = 4
        for r0 in range(UPDATED[t][0], UPDATED[t][1], step):
            n = min(step, UPDATED[t][1] - r0)
            lane = iota((n, 8, 128), 2)
            low = lane & 15
            a0 = O_UP + r0
            tiles = [asm[a0 : a0 + n, :, 128 * q : 128 * q + 128] for q in range(4)]
            ahead = [turn(v, 1) for v in tiles]
            back = [turn(v, -1) for v in tiles]
            new = []
            for q in range(4):
                before = jnp.where(lane == 0, ahead[(q + 3) % 4], ahead[q])
                after = jnp.where(lane == 127, back[(q + 1) % 4], back[q])
                more = jnp.where(low == 0, before, jnp.where(low == 15, after, 0.0))
                if q == 3:
                    pair = jnp.where(lane >= 96, lane - 96, lane)
                    more = jnp.where((pair == 14) | (pair == 15), turn(tiles[3], -2), more)
                    more = jnp.where((pair == 16) | (pair == 17), turn(tiles[3], 2), more)
                cols = slice(128 * q, 128 * q + 128)
                rhs = oi[a0 : a0 + n, :, cols]
                inv = jnp.broadcast_to(oi[a0 : a0 + n, COMP : COMP + 1, cols], (n, 8, 128))
                new.append(rhs - (tiles[q] + more) * inv)
            if t < 3:
                new[0], new[3] = fill(new[0], new[3])
            for q in range(4):
                state[UP + r0 : UP + r0 + n, :, 128 * q : 128 * q + 128] = new[q]

    CH = 512
    for c in loads[6:]:
        c.wait()
    node = node_ref[...]
    node_row = lax.div(node, jnp.int32(COLS))
    e_col = node - node_row * COLS + 3
    e_lane = jnp.where(e_col < 375, e_col + lax.div(e_col, jnp.int32(15)), e_col + 26)

    def setup_rows():
        live = iota((1, IF_CAP), 1) < count_ref[...]
        dest = jnp.where(live, dest_ref[...], -1)
        tri = onehot(iota((256, 256), 0) < iota((256, 256), 1))
        carry = jnp.zeros((D, 1), F32)
        for b in range(IF_CAP // 256):
            cols = slice(256 * b, 256 * b + 256)
            hot = jnp.where(dest[:, cols] == iota((D, 256), 0), 1.0, 0.0)
            desthot[:, cols] = hot.astype(BF16)
            before = mm(hot.astype(BF16), tri) + carry
            slot_s[:, cols] = jnp.sum(before * hot, axis=0, keepdims=True)
            carry = carry + jnp.sum(hot, axis=1, keepdims=True)
        for b in range(IF_CAP // CH):
            cols = slice(CH * b, CH * b + CH)
            colhot[:, cols] = onehot(e_lane[:, cols] == iota((LANES, CH), 0))

    def gather(t):
        lane = iota((1, 256), 1)
        trac = []
        for k in range(3):
            row = jnp.zeros((1, 256), F32)
            for c in range(COMP):
                row = jnp.where((lane & 7) == c, tm_ref[k : k + 1, c : c + 1], row)
            trac.append(jnp.where((iota((32, 256), 1) >> 3) == iota((32, 256), 0), row, 0.0))
        trac = jnp.concatenate(trac, axis=0)
        own = state[UP : UP + ROWS].reshape(ROWS * 8, LANES)
        field = jnp.dot(trac, own, precision=lax.Precision.HIGHEST, preferred_element_type=F32)
        field = jnp.concatenate(pieces(field, 2), axis=0)
        acc = jnp.zeros((D, 128), F32)
        for b in range(IF_CAP // CH):
            cols = slice(CH * b, CH * b + CH)
            v = mm(field, colhot[:, cols])
            v = (v[:96] + v[96:]).reshape(3, 32, CH)
            v = jnp.where(node_row[:, cols][None] == iota((3, 32, CH), 1), v, 0.0)
            v = jnp.sum(v, axis=1, keepdims=True)
            v = jnp.concatenate([v, target_ref[:, cols].astype(F32)[None]], axis=0)
            slots = slot_s[:, cols].astype(jnp.int32)[None] == iota((4, CAP, CH), 1)
            v = jnp.where(slots, v, 0.0).reshape(4 * CAP, CH)
            for p in pieces(v, 2):
                acc = acc + mm_nt(desthot[:, cols], p)
        abuf[t] = acc.reshape(D // 8, 8, 128)

    def a2a_1(t):
        copies = []
        for o, (dg, dx) in enumerate(gx_partners):
            to_g, to_s = at_gx(dg, dx)
            copies.append(
                pltpu.make_async_remote_copy(
                    src_ref=abuf.at[t, to_g * X + to_s // W],
                    dst_ref=r1.at[t, pl.ds(8 * (o + 1), 8)],
                    send_sem=a1_send.at[t, o],
                    recv_sem=a1_recv.at[t, o],
                    device_id=(to_g, to_s),
                    device_id_type=MESH,
                )
            )
            copies[-1].start()
        r1[t, 0:8] = abuf[t, g * X + x]
        return copies

    def a2a_2(t, first):
        for c in first:
            c.wait_recv()
        for d in range(W):
            r1t[t, d] = r1[t, pl.ds(d, D // W, stride=W), :]
        copies = []
        for dw in range(1, W):
            to = at_w(dw)
            copies.append(
                pltpu.make_async_remote_copy(
                    src_ref=r1t.at[t, lax.rem(w + dw, W)],
                    dst_ref=r3.at[t, dw],
                    send_sem=a2_send.at[t, dw - 1],
                    recv_sem=a2_recv.at[t, dw - 1],
                    device_id=to,
                    device_id_type=MESH,
                )
            )
            copies[-1].start()
        r3[t, 0] = r1t[t, w]
        return copies

    def place(t, second):
        for c in second:
            c.wait_recv()
        got = r3[t].reshape(D, 128).T
        name = got[96:128]
        high = jnp.floor(name * (1.0 / 128.0))
        low = name - 128.0 * high
        acc = jnp.zeros((96, 128), F32)
        for q in range(CAP // 4):
            left, right = [], []
            for z in range(4 * q, 4 * q + 4):
                right.append(onehot(low[z : z + 1] == iota((128, D), 0).astype(F32)))
                hit = high[z : z + 1] == iota((16, D), 0).astype(F32)
                v = jnp.concatenate(
                    [jnp.where(hit, got[32 * k + z : 32 * k + z + 1], 0.0) for k in range(3)], axis=0
                )
                left.append(jnp.concatenate(pieces(v, 2), axis=0))
            acc = acc + mm_nt(jnp.concatenate(left, axis=1), jnp.concatenate(right, axis=1))
        acc = acc[:48] + acc[48:]
        for k in range(3):
            for h in range(16):
                load_ref[t, k : k + 1, 128 * h : 128 * h + 128] = acc[16 * k + h : 16 * k + h + 1]

    def write_adjoint():
        own = state[UP : UP + ROWS].reshape(ROWS * 8, LANES)
        lane = iota((LANES, COLS), 0)
        j, b = lane >> 4, lane & 15
        keep = ((j < 25) & (b < 15)) | ((j == 25) & (b > 0))
        back = onehot(keep & (ext_col(lane) == iota((LANES, COLS), 1) + 3))
        n = iota((COMP * ROWS, ROWS * 8), 1)
        unperm = onehot((n & 7) * ROWS + (n >> 3) == iota((COMP * ROWS, ROWS * 8), 0))
        out_ref[...] = pick_rows(unperm, pick(own, back)).reshape(COMP, ROWS, COLS)

    setup_rows()
    sides_finish()
    row_late = row_copies(10, slice(384, 512))
    for c in row_late:
        c.start()
    fill_rows(UP, ROWS - DOWN - 1)
    for c in row_early + row_late:
        c.wait_recv()
    for c in row_late + row_early:
        c.wait_send()
    fill_rows(-UP, UP)
    fill_rows(ROWS - DOWN - 1, ROWS + DOWN)
    sweep(0)
    sweep(1)
    gather(0)
    first = a2a_1(0)
    sent = side_copies + first
    sweep(2)
    second = a2a_2(0, first)
    sent += second
    sweep(3)
    gather(1)
    first = a2a_1(1)
    sent += first
    place(0, second)
    second = a2a_2(1, first)
    sent += second
    write_adjoint()
    place(1, second)
    for c in sent:
        c.wait_send()


def on_device(
    G,
    S,
    adjoint_start,
    objective_grad,
    diagonal,
    connect,
    element_scale,
    element_matrix,
    traction_map,
    iface_node,
    iface_dest,
    iface_target,
    iface_count,
):
    vmem = pl.BlockSpec(memory_space=pltpu.VMEM)
    D = G * S
    XG = D // W
    dma = pltpu.SemaphoreType.DMA
    I32 = jnp.int32
    scratch = [
        pltpu.VMEM((COMP, ROWS, COLS), F32),
        pltpu.VMEM((COMP, ROWS, COLS), F32),
        pltpu.VMEM((ROWS, COLS), F32),
        pltpu.VMEM((8, ELEMS), I32),
        pltpu.VMEM((64, ELEMS), F32),
        pltpu.VMEM((64, 64), BF16),
        pltpu.VMEM((3, COMP), F32),
        pltpu.VMEM((1, IF_CAP), I32),
        pltpu.VMEM((1, IF_CAP), I32),
        pltpu.VMEM((1, IF_CAP), I32),
        pltpu.VMEM((1, 1), I32),
        dma((11,)),
        pltpu.VMEM((UP + ROWS + DOWN, 8, LANES), F32),
        pltpu.VMEM((O_UP + ROWS + O_DOWN, 8, LANES), F32),
        pltpu.VMEM((O_UP + ROWS + O_DOWN, 8, LANES), F32),
        pltpu.VMEM((4, 16, LANES), F32),
        pltpu.VMEM((4, 8, LANES), F32),
        pltpu.VMEM((4, 8, LANES), F32),
        pltpu.VMEM((LANES, LANES), BF16),
        pltpu.VMEM((8, 384), I32),
        pltpu.VMEM((64, 384), F32),
        pltpu.VMEM((LANES, IF_CAP), BF16),
        pltpu.VMEM((D, IF_CAP), BF16),
        pltpu.VMEM((1, IF_CAP), F32),
        pltpu.VMEM((2, ROWS, 8, 128), F32),
        pltpu.VMEM((2, ROWS, 8, 128), F32),
        pltpu.VMEM((2, 4, 16, 128), F32),
        pltpu.VMEM((2, 4, 16, 128), F32),
        pltpu.VMEM((ITERS, XG, 8, 128), F32),
        pltpu.VMEM((ITERS, D, 128), F32),
        pltpu.VMEM((ITERS, W, XG, 128), F32),
        pltpu.VMEM((ITERS, W, XG, 128), F32),
        dma((16,)),
        dma((16,)),
        dma((ITERS, XG - 1)),
        dma((ITERS, XG - 1)),
        dma((ITERS, W - 1)),
        dma((ITERS, W - 1)),
    ]
    call = pl.pallas_call(
        functools.partial(kernel, G, S),
        out_shape=(
            jax.ShapeDtypeStruct((COMP, ROWS, COLS), F32),
            jax.ShapeDtypeStruct((ITERS, 3, IF_CAP), F32),
        ),
        in_specs=[pl.BlockSpec(memory_space=pl.ANY)] * 11,
        out_specs=(vmem, vmem),
        scratch_shapes=scratch,
        compiler_params=pltpu.CompilerParams(
            collective_id=0, has_side_effects=True, vmem_limit_bytes=48 * 1024 * 1024
        ),
    )
    return call(
        adjoint_start,
        objective_grad,
        diagonal,
        connect,
        element_scale,
        element_matrix,
        traction_map,
        iface_node.reshape(1, IF_CAP),
        iface_dest.reshape(1, IF_CAP),
        iface_target.reshape(1, IF_CAP),
        iface_count.reshape(1, 1),
    )


def solution(mesh):
    both = ("group", "sub")
    placed = (
        P(None, "group", "sub"),
        P(None, "group", "sub"),
        P("group", "sub"),
        P(None, both),
        P(None, both),
        P(),
        P(),
        P(both),
        P(both, None),
        P(both),
        P(both),
    )
    return jax.shard_map(
        functools.partial(on_device, mesh.shape["group"], mesh.shape["sub"]),
        mesh=mesh,
        in_specs=placed,
        out_specs=(P(None, "group", "sub"), P(None, None, both)),
        check_vma=False,
    )
```

time: 54.2 us -> 51.1 us (0.943)
  Pallas kernels: 43 us -> 40.6 us
  local copies, waits for them, and re-layouts: 9.36 us -> 8.7 us
    pallas_call x1, Pallas kernels: 43 us -> 40.6 us  [on_device(): call(adjoint_start, objective_grad, diagonal, connect, element_scale, ele...]
    unnamed x21, local copies, waits for them, and re-layouts: 8.7 us -> 8.04 us
where the time goes in v2:
time: 51.1 us; the launch traced here: 50.6 us
  Pallas kernels  40.6 us (79%)
  local copies, waits for them, and re-layouts  8.7 us (17%)
  between operations  1.32 us (3%)
    pallas_call x1, Pallas kernels, on_device(): call(adjoint_start, objective_grad, diagonal, connect, element_scale, ele...  40.6 us
    unnamed x21, local copies, waits for them, and re-layouts  8.04 us

profile of v2, /device:TPU:1, one launch (start us, length us, event | category | flops | bytes accessed | tf_op | source)
XLA Modules:
  0.0 50.6 jit_solution(9372576116474488026)
XLA Ops:
  0.6 0.0 copy-start.6
  1.3 0.0 copy-done.6
  1.3 0.0 copy-start
  1.3 1.0 %copy-done = f32[6,32,384]{2,1,0:T(8,128)S(1)} copy-done((f32[6,32,384]{2,1,0:T(8,128)S(1)}, f32[6,32,384]{2,1,0:T(8,128)}, u32[]{:S(2)}) %copy-start) | copy-done | bytes 294936
  2.3 0.0 copy-start.1
  2.3 1.0 %copy-done.1 = f32[6,32,384]{2,1,0:T(8,128)S(1)} copy-done((f32[6,32,384]{2,1,0:T(8,128)S(1)}, f32[6,32,384]{2,1,0:T(8,128)}, u32[]{:S(2)}) %copy-start.1) | copy-done | bytes 294936
  3.3 0.0 copy-start.2
  3.3 0.9 %copy-done.2 = s32[64,338]{1,0:T(8,128)S(1)} copy-done((s32[64,338]{1,0:T(8,128)S(1)}, s32[64,338]{1,0:T(8,128)}, u32[]{:S(2)}) %copy-start.2) | copy-done | bytes 86552
  4.1 0.0 copy-start.3
  4.2 0.9 %copy-done.3 = f32[64,338]{1,0:T(8,128)S(1)} copy-done((f32[64,338]{1,0:T(8,128)S(1)}, f32[64,338]{1,0:T(8,128)}, u32[]{:S(2)}) %copy-start.3) | copy-done | bytes 86552
  5.0 0.0 copy-start.4
  5.0 0.8 %copy-done.4 = f32[32,384]{1,0:T(8,128)S(1)} copy-done((f32[32,384]{1,0:T(8,128)S(1)}, f32[32,384]{1,0:T(8,128)}, u32[]{:S(2)}) %copy-start.4) | copy-done | bytes 49176
  5.8 0.0 copy-start.5
  5.8 0.7 %copy-done.5 = bf16[64,64]{1,0:T(8,128)(2,1)S(1)} copy-done((bf16[64,64]{1,0:T(8,128)(2,1)S(1)}, bf16[64,64]{1,0:T(8,128)(2,1)}, u32[]{:S(2)}) %copy-start.5) | copy-done | bytes 8216
  6.6 0.0 copy-start.7
  6.6 0.7 %copy-done.7 = s32[2048,1]{0,1:T(1,128)S(1)} copy-done((s32[2048,1]{0,1:T(1,128)S(1)}, s32[2048,1]{0,1:T(1,128)}, u32[]{:S(2)}) %copy-start.7) | copy-done | bytes 8216
  7.3 0.0 copy-start.8
  7.3 0.7 %copy-done.8 = s32[2048]{0:T(1024)S(1)} copy-done((s32[2048]{0:T(1024)S(1)}, s32[2048]{0:T(1024)}, u32[]{:S(2)}) %copy-start.8) | copy-done | bytes 8216
  8.0 0.0 copy-start.9
  8.0 0.7 %copy-done.9 = f32[3,6]{1,0:T(4,128)S(1)} copy-done((f32[3,6]{1,0:T(4,128)S(1)}, f32[3,6]{1,0:T(4,128)}, u32[]{:S(2)}) %copy-start.9) | copy-done | bytes 96
  8.6 40.6 %shard_map.122 = (f32[6,32,384]{2,1,0:T(8,128)S(1)}, f32[2,3,2048]{2,1,0:T(4,128)S(1)}) custom-call(f32[6,32,384]{2,1,0:T(8,128)S(1)} %copy-done, f32[6,32,384]{2,1,0:T(8,128)S(1)} %copy-done.1, f32[32,384]{1,0:T(8,128)S(1)} %copy-done.4, s32[64,338]{1,0:T(8,128)S(1)} %copy-done.2, f32[64,338]{1,0:T(8,128)S(1)} %copy-done.3, bf16[64,64]{1,0:T(8,128)(2,1)S(1)} %copy-done.5, ...), custom_call_target="tpu_custom_call" | custom-call | tf_op jit(solution)/shard_map/pallas_call | solution.py:626
  49.2 0.7 %copy.13 = f32[2,3,2048]{2,0,1:T(2,128)} copy(f32[2,3,2048]{2,1,0:T(4,128)S(1)} %get-tuple-element.3) | data formatting | bytes 98304 | tf_op jit(solution)/shard_map/pallas_call | solution.py:626
  49.9 0.7 %copy.16 = f32[6,32,384]{2,1,0:T(8,128)} copy(f32[6,32,384]{2,1,0:T(8,128)S(1)} %get-tuple-element.6) | data formatting | bytes 589824
Async XLA Ops:
  0.6 0.7 %copy-start.6 = (s32[2048]{0:T(1024)S(1)}, s32[2048]{0:T(1024)}, u32[]{:S(2)}) copy-start(s32[2048]{0:T(1024)} %param.18) | copy-start | bytes 24580
  1.3 1.0 %copy-start = (f32[6,32,384]{2,1,0:T(8,128)S(1)}, f32[6,32,384]{2,1,0:T(8,128)}, u32[]{:S(2)}) copy-start(f32[6,32,384]{2,1,0:T(8,128)} %adj_hbm.1) | copy-start | bytes 884740
  2.3 1.0 %copy-start.1 = (f32[6,32,384]{2,1,0:T(8,128)S(1)}, f32[6,32,384]{2,1,0:T(8,128)}, u32[]{:S(2)}) copy-start(f32[6,32,384]{2,1,0:T(8,128)} %obj_hbm.1) | copy-start | bytes 884740
  3.3 0.9 %copy-start.2 = (s32[64,338]{1,0:T(8,128)S(1)}, s32[64,338]{1,0:T(8,128)}, u32[]{:S(2)}) copy-start(s32[64,338]{1,0:T(8,128)} %conn_hbm.1) | copy-start | bytes 259588
  4.1 0.9 %copy-start.3 = (f32[64,338]{1,0:T(8,128)S(1)}, f32[64,338]{1,0:T(8,128)}, u32[]{:S(2)}) copy-start(f32[64,338]{1,0:T(8,128)} %scale_hbm.1) | copy-start | bytes 259588
  5.0 0.8 %copy-start.4 = (f32[32,384]{1,0:T(8,128)S(1)}, f32[32,384]{1,0:T(8,128)}, u32[]{:S(2)}) copy-start(f32[32,384]{1,0:T(8,128)} %diag_hbm.1) | copy-start | bytes 147460
  5.8 0.7 %copy-start.5 = (bf16[64,64]{1,0:T(8,128)(2,1)S(1)}, bf16[64,64]{1,0:T(8,128)(2,1)}, u32[]{:S(2)}) copy-start(bf16[64,64]{1,0:T(8,128)(2,1)} %em_hbm.1) | copy-start | bytes 24580
  6.6 0.7 %copy-start.7 = (s32[2048,1]{0,1:T(1,128)S(1)}, s32[2048,1]{0,1:T(1,128)}, u32[]{:S(2)}) copy-start(s32[2048,1]{0,1:T(1,128)} %param.19) | copy-start | bytes 24580
  7.3 0.7 %copy-start.8 = (s32[2048]{0:T(1024)S(1)}, s32[2048]{0:T(1024)}, u32[]{:S(2)}) copy-start(s32[2048]{0:T(1024)} %param.20) | copy-start | bytes 24580
  8.0 0.7 %copy-start.9 = (f32[3,6]{1,0:T(4,128)S(1)}, f32[3,6]{1,0:T(4,128)}, u32[]{:S(2)}) copy-start(f32[3,6]{1,0:T(4,128)} %tm_hbm.1) | copy-start | bytes 220

commit v3 on v2

--- a/solution.py
+++ b/solution.py
@@ -201,6 +201,63 @@
     first = pick_rows(perm, scaled_obj) + pick_rows(perm_inv, inverse)
     oi[O_UP : O_UP + ROWS] = pick(first, sel).reshape(ROWS, 8, LANES)
 
+    def remote(n, src, dst, dev):
+        return pltpu.make_async_remote_copy(
+            src_ref=src,
+            dst_ref=dst,
+            send_sem=halo_send.at[n],
+            recv_sem=halo_recv.at[n],
+            device_id=dev,
+            device_id_type=MESH,
+        )
+
+    def turn(v, n):
+        return pltpu.roll(v, n % 128, v.ndim - 1)
+
+    def pack_right(two, three, start):
+        lane = iota(two.shape, two.ndim - 1)
+        return jnp.where(lane < start + 16, turn(two, start - 112), turn(three, start + 16))
+
+    for p in range(0, ROWS, 8):
+        st = [state[UP + p : UP + p + 8, :, 128 * q : 128 * q + 128] for q in (0, 2, 3)]
+        ob = [oi[O_UP + p : O_UP + p + 8, :, 128 * q : 128 * q + 128] for q in (0, 2, 3)]
+        lane = iota((8, 8, 128), 2)
+        side_send[0, p : p + 8] = jnp.where(lane < 80, turn(st[0], 32), turn(ob[0], 80))
+        side_send[1, p : p + 8] = jnp.where(
+            lane < 80, pack_right(ob[1], ob[2], 32), pack_right(st[1], st[2], 80)
+        )
+    def row_copies(n, cols):
+        up, down = at(-1, 0), at(1, 0)
+        return [
+            remote(n, state.at[UP + ROWS - UP : UP + ROWS, :, cols], state.at[0:UP, :, cols], down),
+            remote(
+                n + 1,
+                state.at[UP : UP + DOWN, :, cols],
+                state.at[UP + ROWS : UP + ROWS + DOWN, :, cols],
+                up,
+            ),
+            remote(n + 2, oi.at[ROWS : O_UP + ROWS, :, cols], oi.at[0:O_UP, :, cols], down),
+            remote(
+                n + 3,
+                oi.at[O_UP : O_UP + O_DOWN, :, cols],
+                oi.at[O_UP + ROWS : O_UP + ROWS + O_DOWN, :, cols],
+                up,
+            ),
+            remote(n + 4, scale_own.at[:, 8:16, cols], scale_up.at[:, :, cols], down),
+            remote(n + 5, scale_own.at[:, 0:8, cols], scale_down.at[:, :, cols], up),
+        ]
+
+    pl.semaphore_wait(barrier, len(targets))
+    side_copies = [
+        remote(0, side_send.at[0], side_recv.at[0], at(0, -1)),
+        remote(1, side_send.at[1], side_recv.at[1], at(0, 1)),
+        remote(2, sscale_send.at[0], sscale_recv.at[0], at(0, -1)),
+        remote(3, sscale_send.at[1], sscale_recv.at[1], at(0, 1)),
+    ]
+    row_early = row_copies(4, slice(0, 384))
+    for c in side_copies[:2] + row_early[:4]:
+        c.start()
+
     loads[3].wait()
     loads[4].wait()
     conn_pad[...] = jnp.full_like(conn_pad, -1)
@@ -226,68 +283,10 @@
         r = start_row + a
         off = ((g == 0) & (r < 3)) | ((g == G - 1) & (r >= ROWS + 3)) | off_side
         scale_own[a] = jnp.where(off, 0.0, total(out))
-
-    def remote(n, src, dst, dev):
-        return pltpu.make_async_remote_copy(
-            src_ref=src,
-            dst_ref=dst,
-            send_sem=halo_send.at[n],
-            recv_sem=halo_recv.at[n],
-            device_id=dev,
-            device_id_type=MESH,
-        )
-
-    def turn(v, n):
-        return pltpu.roll(v, n % 128, v.ndim - 1)
-
-    def pack_right(two, three, start):
-        lane = iota(two.shape, two.ndim - 1)
-        return jnp.where(lane < start + 16, turn(two, start - 112), turn(three, start + 16))
-
-    for p in range(0, ROWS, 8):
-        st = [state[UP + p : UP + p + 8, :, 128 * q : 128 * q + 128] for q in (0, 2, 3)]
-        ob = [oi[O_UP + p : O_UP + p + 8, :, 128 * q : 128 * q + 128] for q in (0, 2, 3)]
-        lane = iota((8, 8, 128), 2)
-        side_send[0, p : p + 8] = jnp.where(lane < 80, turn(st[0], 32), turn(ob[0], 80))
-        side_send[1, p : p + 8] = jnp.where(
-            lane < 80, pack_right(ob[1], ob[2], 32), pack_right(st[1], st[2], 80)
-        )
     for a in range(4):
         sscale_send[0, a] = turn(scale_own[a, :, 0:128], 32)
         sscale_send[1, a] = pack_right(scale_own[a, :, 256:384], scale_own[a, :, 384:512], 80)
-
-    def row_copies(n, cols):
-        up, down = at(-1, 0), at(1, 0)
-        return [
-            remote(n, state.at[UP + ROWS - UP : UP + ROWS, :, cols], state.at[0:UP, :, cols], down),
-            remote(
-                n + 1,
-                state.at[UP : UP + DOWN, :, cols],
-                state.at[UP + ROWS : UP + ROWS + DOWN, :, cols],
-                up,
-            ),
-            remote(n + 2, oi.at[ROWS : O_UP + ROWS, :, cols], oi.at[0:O_UP, :, cols], down),
-            remote(
-                n + 3,
-                oi.at[O_UP : O_UP + O_DOWN, :, cols],
-                oi.at[O_UP + ROWS : O_UP + ROWS + O_DOWN, :, cols],
-                up,
-            ),
-            remote(n + 4, scale_own.at[:, 8:16, cols], scale_up.at[:, :, cols], down),
-            remote(n + 5, scale_own.at[:, 0:8, cols], scale_down.at[:, :, cols], up),
-        ]
-
-    pl.semaphore_wait(barrier, len(targets))
-    side_copies = [
-        remote(0, side_send.at[0], side_recv.at[0], at(0, -1)),
-        remote(1, side_send.at[1], side_recv.at[1], at(0, 1)),
-        remote(2, sscale_send.at[0], sscale_recv.at[0], at(0, -1)),
-        remote(3, sscale_send.at[1], sscale_recv.at[1], at(0, 1)),
-    ]
-    for c in side_copies:
-        c.start()
-    row_early = row_copies(4, slice(0, 384))
-    for c in row_early:
+    for c in side_copies[2:] + row_early[4:]:
         c.start()
 
     loads[5].wait()
@@ -532,21 +531,17 @@
     sweep(0)
     sweep(1)
     gather(0)
-    first = a2a_1(0)
-    sent = side_copies + first
+    first_0 = a2a_1(0)
     sweep(2)
-    second = a2a_2(0, first)
-    sent += second
     sweep(3)
     gather(1)
-    first = a2a_1(1)
-    sent += first
-    place(0, second)
-    second = a2a_2(1, first)
-    sent += second
+    first_1 = a2a_1(1)
+    second_0 = a2a_2(0, first_0)
     write_adjoint()
-    place(1, second)
-    for c in sent:
+    second_1 = a2a_2(1, first_1)
+    place(0, second_0)
+    place(1, second_1)
+    for c in side_copies + first_0 + first_1 + second_0 + second_1:
         c.wait_send()
 
 
@@ -620,7 +615,7 @@
         out_specs=(vmem, vmem),
         scratch_shapes=scratch,
         compiler_params=pltpu.CompilerParams(
-            collective_id=0, has_side_effects=True, vmem_limit_bytes=48 * 1024 * 1024
+            collective_id=0, has_side_effects=True, vmem_limit_bytes=62 * 1024 * 1024
         ),
     )
     return call(

time: 51.1 us -> 40.7 us (0.80)
  local copies, waits for them, and re-layouts: 8.7 us -> 3.19 us
  Pallas kernels: 40.6 us -> 36 us
    unnamed x21 -> x1, local copies, waits for them, and re-layouts: 8.04 us -> 1.69 us
    pallas_call x1, Pallas kernels: 40.6 us -> 36 us  [on_device(): call(adjoint_start, objective_grad, diagonal, connect, element_scale, ele...]
    pallas_call x1, local copies, waits for them, and re-layouts: 0.66 us -> 1.5 us  [on_device(): call(adjoint_start, objective_grad, diagonal, connect, element_scale, ele...]
where the time goes in v3:
time: 40.7 us; the launch traced here: 40.5 us
  Pallas kernels  36 us (88%)
  local copies, waits for them, and re-layouts  3.19 us (8%)
  between operations  1.29 us (3%)
    pallas_call x1, Pallas kernels, on_device(): call(adjoint_start, objective_grad, diagonal, connect, element_scale, ele...  36 us
    unnamed x1, local copies, waits for them, and re-layouts  1.69 us
    pallas_call x1, local copies, waits for them, and re-layouts, on_device(): call(adjoint_start, objective_grad, diagonal, connect, element_scale, ele...  1.5 us

profile of v3, /device:TPU:1, one launch (start us, length us, event | category | flops | bytes accessed | tf_op | source)
XLA Modules:
  0.0 40.5 jit_solution(16260059329801552062)
XLA Ops:
  1.3 36.0 %shard_map.122 = (f32[6,32,384]{2,1,0:T(8,128)}, f32[2,3,2048]{2,1,0:T(4,128)}) custom-call(f32[6,32,384]{2,1,0:T(8,128)} %adj_hbm.1, f32[6,32,384]{2,1,0:T(8,128)} %obj_hbm.1, f32[32,384]{1,0:T(8,128)} %diag_hbm.1, s32[64,338]{1,0:T(8,128)} %conn_hbm.1, f32[64,338]{1,0:T(8,128)} %scale_hbm.1, bf16[64,64]{1,0:T(8,128)(2,1)} %em_hbm.1, f32[3,6]{1,0:T(4,128)} %tm_hbm.1, ...), custom_call_target="tpu_custom_call" | custom-call | tf_op jit(solution)/shard_map/pallas_call | solution.py:621
  37.3 1.5 %copy.13 = f32[2,3,2048]{2,0,1:T(2,128)} copy(f32[2,3,2048]{2,1,0:T(4,128)} %get-tuple-element.3) | data formatting | bytes 98304 | tf_op jit(solution)/shard_map/pallas_call | solution.py:621
  38.8 1.7 %copy.16 = f32[6,32,384]{2,1,0:T(8,128)} copy(f32[6,32,384]{2,1,0:T(8,128)} %get-tuple-element.6) | data formatting | bytes 589824

commit v4 on v3

--- a/solution.py
+++ b/solution.py
@@ -22,7 +22,6 @@
 )
 ACTIVE = [(0, 22), (1, 21), (2, 20), (4, 18)]
 UPDATED = [(-8, 39), (-5, 36), (-3, 35), (0, 32)]
-W = 8
 F32 = jnp.float32
 BF16 = jnp.bfloat16
 MESH = pl.DeviceIdType.MESH
@@ -100,8 +99,11 @@
     dest_hbm,
     target_hbm,
     count_hbm,
+    out_hbm,
+    load_hbm,
     out_ref,
     load_ref,
+    out_sem,
     adj_ref,
     obj_ref,
     diag_ref,
@@ -114,7 +116,9 @@
     target_ref,
     count_ref,
     in_sem,
-    state,
+    state_a,
+    state_b,
+    field_s,
     oi,
     asm,
     scale_own,
@@ -131,31 +135,20 @@
     sscale_send,
     sscale_recv,
     abuf,
-    r1,
-    r1t,
-    r3,
+    arrived,
     halo_send,
     halo_recv,
-    a1_send,
-    a1_recv,
-    a2_send,
-    a2_recv,
+    all_send,
+    all_recv,
 ):
-    X = S // W
     D = G * S
+    states = (state_a, state_b)
+    state = state_a
     g = lax.axis_index("group")
     s = lax.axis_index("sub")
-    x = s // W
-    w = s % W
 
     def at(dg, ds):
         return (lax.rem(g + dg + G, G), lax.rem(s + ds + S, S))
-
-    def at_gx(dg, dx):
-        return (lax.rem(g + dg, G), lax.rem(x + dx, X) * W + w)
-
-    def at_w(dw):
-        return (g, x * W + lax.rem(w + dw, W))
 
     loads = [
         pltpu.make_async_copy(src, dst, in_sem.at[n])
@@ -177,11 +170,9 @@
     ]
     for c in loads:
         c.start()
-    gx_partners = [(dg, dx) for dg in range(G) for dx in range(X)][1:]
     barrier = pltpu.get_barrier_semaphore()
-    targets = [at(0, -1), at(0, 1)]
-    targets += [at_gx(*p) for p in gx_partners] + [at_w(dw) for dw in range(1, W)]
-    for t in targets:
+    others = [at(dg, ds) for ds in range(S) for dg in range(G)][1:]
+    for t in others:
         pl.semaphore_signal(barrier, inc=1, device_id=t, device_id_type=MESH)
 
     lane = iota((COLS, LANES), 1)
@@ -226,37 +217,32 @@
         side_send[1, p : p + 8] = jnp.where(
             lane < 80, pack_right(ob[1], ob[2], 32), pack_right(st[1], st[2], 80)
         )
-    def row_copies(n, cols):
-        up, down = at(-1, 0), at(1, 0)
+    def pair(n, ref, up_to, down_rows, up_rows, cols):
+        lo, hi = down_rows
+        first, last = up_rows
         return [
-            remote(n, state.at[UP + ROWS - UP : UP + ROWS, :, cols], state.at[0:UP, :, cols], down),
+            remote(n, ref.at[lo:hi, :, cols], ref.at[0 : hi - lo, :, cols], at(1, 0)),
             remote(
                 n + 1,
-                state.at[UP : UP + DOWN, :, cols],
-                state.at[UP + ROWS : UP + ROWS + DOWN, :, cols],
-                up,
+                ref.at[first:last, :, cols],
+                ref.at[up_to : up_to + last - first, :, cols],
+                at(-1, 0),
             ),
-            remote(n + 2, oi.at[ROWS : O_UP + ROWS, :, cols], oi.at[0:O_UP, :, cols], down),
-            remote(
-                n + 3,
-                oi.at[O_UP : O_UP + O_DOWN, :, cols],
-                oi.at[O_UP + ROWS : O_UP + ROWS + O_DOWN, :, cols],
-                up,
-            ),
-            remote(n + 4, scale_own.at[:, 8:16, cols], scale_up.at[:, :, cols], down),
-            remote(n + 5, scale_own.at[:, 0:8, cols], scale_down.at[:, :, cols], up),
         ]
 
-    pl.semaphore_wait(barrier, len(targets))
-    side_copies = [
-        remote(0, side_send.at[0], side_recv.at[0], at(0, -1)),
-        remote(1, side_send.at[1], side_recv.at[1], at(0, 1)),
-        remote(2, sscale_send.at[0], sscale_recv.at[0], at(0, -1)),
-        remote(3, sscale_send.at[1], sscale_recv.at[1], at(0, 1)),
-    ]
-    row_early = row_copies(4, slice(0, 384))
-    for c in side_copies[:2] + row_early[:4]:
-        c.start()
+    def state_rows(n, cols):
+        return pair(n, state, UP + ROWS, (ROWS, UP + ROWS), (UP, UP + DOWN), cols)
+
+    def oi_rows(n, cols):
+        return pair(
+            n, oi, O_UP + ROWS, (ROWS, O_UP + ROWS), (O_UP, O_UP + O_DOWN), cols
+        )
+
+    def scale_rows(n, cols):
+        return [
+            remote(n, scale_own.at[:, 8:16, cols], scale_up.at[:, :, cols], at(1, 0)),
+            remote(n + 1, scale_own.at[:, 0:8, cols], scale_down.at[:, :, cols], at(-1, 0)),
+        ]
 
     loads[3].wait()
     loads[4].wait()
@@ -286,7 +272,16 @@
     for a in range(4):
         sscale_send[0, a] = turn(scale_own[a, :, 0:128], 32)
         sscale_send[1, a] = pack_right(scale_own[a, :, 256:384], scale_own[a, :, 384:512], 80)
-    for c in side_copies[2:] + row_early[4:]:
+    pl.semaphore_wait(barrier, len(others))
+    side_copies = [
+        remote(0, side_send.at[0], side_recv.at[0], at(0, -1)),
+        remote(1, side_send.at[1], side_recv.at[1], at(0, 1)),
+        remote(2, sscale_send.at[0], sscale_recv.at[0], at(0, -1)),
+        remote(3, sscale_send.at[1], sscale_recv.at[1], at(0, 1)),
+    ]
+    early, last_tile = slice(0, 384), slice(384, 512)
+    row_early = state_rows(4, slice(128, 384)) + oi_rows(6, early) + scale_rows(8, early)
+    for c in side_copies + row_early:
         c.start()
 
     loads[5].wait()
@@ -329,11 +324,11 @@
         three_new = jnp.where(lane >= 125, turn(first, -6), three_new)
         return first_new, three_new
 
-    def fill_rows(lo, hi):
-        lo, hi = UP + lo, UP + hi
-        state[lo:hi, :, 0:128], state[lo:hi, :, 384:512] = fill(
-            state[lo:hi, :, 0:128], state[lo:hi, :, 384:512]
-        )
+    def fill_rows():
+        for r in range(UP, UP + ROWS, 8):
+            state[r : r + 8, :, 0:128], state[r : r + 8, :, 384:512] = fill(
+                state[r : r + 8, :, 0:128], state[r : r + 8, :, 384:512]
+            )
 
     def scale_row(a, e, cols):
         if e < 5:
@@ -344,31 +339,31 @@
             v = scale_down[a, e - 18 : e - 17, cols]
         return jnp.broadcast_to(v, (8, 128))
 
-    def sweep(t):
-        lo, hi = ACTIVE[t]
-        rows = range(*UPDATED[t])
-        count = hi - lo
+    def products(t, elems, rows, begun=()):
+        src = states[t % 2]
         for q in range(4):
             cols = slice(128 * q, 128 * q + 128)
             parts = []
             for a in range(4):
-                v = [
-                    state[UP + STARTS[e] + a, :, cols] * scale_row(a, e, cols)
-                    for e in range(lo, hi)
-                ]
+                v = [src[UP + STARTS[e] + a, :, cols] * scale_row(a, e, cols) for e in elems]
                 parts.append(jnp.concatenate(v, axis=0).astype(BF16))
             o = mm(jnp.concatenate(parts, axis=1), wmat[...])
             for row in rows:
                 terms = [
-                    o[8 * (e - lo) : 8 * (e - lo) + 8, 128 * a : 128 * a + 128]
-                    for e in range(lo, hi)
+                    o[8 * n : 8 * n + 8, 128 * a : 128 * a + 128]
+                    for n, e in enumerate(elems)
                     for a in range(4)
                     if STARTS[e] + a == row and block_of(e) == owner(row)
                 ]
+                if row in begun:
+                    terms.append(asm[O_UP + row, :, cols])
                 asm[O_UP + row, :, cols] = total(terms)
+
+    def update(t, first, last):
+        dst = states[(t + 1) % 2]
         step = 4
-        for r0 in range(UPDATED[t][0], UPDATED[t][1], step):
-            n = min(step, UPDATED[t][1] - r0)
+        for r0 in range(first, last, step):
+            n = min(step, last - r0)
             lane = iota((n, 8, 128), 2)
             low = lane & 15
             a0 = O_UP + r0
@@ -391,7 +386,24 @@
             if t < 3:
                 new[0], new[3] = fill(new[0], new[3])
             for q in range(4):
-                state[UP + r0 : UP + r0 + n, :, 128 * q : 128 * q + 128] = new[q]
+                dst[UP + r0 : UP + r0 + n, :, 128 * q : 128 * q + 128] = new[q]
+
+    def sweep(t):
+        products(t, range(*ACTIVE[t]), range(*UPDATED[t]))
+        update(t, *UPDATED[t])
+
+    INNER = range(6, 16)
+
+    def sweep_0_inner():
+        products(0, INNER, range(0, 31))
+        update(0, 1, 30)
+
+    def sweep_0_outer():
+        rows = [r for r in range(*UPDATED[0]) if r < 1 or r > 29]
+        products(0, [e for e in range(*ACTIVE[0]) if e not in INNER], rows, (0, 30))
+        update(0, UPDATED[0][0], 1)
+        update(0, 30, UPDATED[0][1])
+
 
     CH = 512
     for c in loads[6:]:
@@ -417,7 +429,7 @@
             cols = slice(CH * b, CH * b + CH)
             colhot[:, cols] = onehot(e_lane[:, cols] == iota((LANES, CH), 0))
 
-    def gather(t):
+    def tractions(t):
         lane = iota((1, 256), 1)
         trac = []
         for k in range(3):
@@ -425,86 +437,78 @@
             for c in range(COMP):
                 row = jnp.where((lane & 7) == c, tm_ref[k : k + 1, c : c + 1], row)
             trac.append(jnp.where((iota((32, 256), 1) >> 3) == iota((32, 256), 0), row, 0.0))
-        trac = jnp.concatenate(trac, axis=0)
+        high, low = pieces(jnp.concatenate(trac, axis=0), 2)
         own = state[UP : UP + ROWS].reshape(ROWS * 8, LANES)
-        field = jnp.dot(trac, own, precision=lax.Precision.HIGHEST, preferred_element_type=F32)
-        field = jnp.concatenate(pieces(field, 2), axis=0)
-        acc = jnp.zeros((D, 128), F32)
+        own_high, own_low = pieces(own, 2)
+        field = mm(high, own_high) + (mm(high, own_low) + mm(low, own_high))
+        field_s[192 * t : 192 * t + 192] = jnp.concatenate(pieces(field, 2), axis=0)
+
+    def gather():
+        acc = jnp.zeros((D, 256), F32)
         for b in range(IF_CAP // CH):
             cols = slice(CH * b, CH * b + CH)
-            v = mm(field, colhot[:, cols])
-            v = (v[:96] + v[96:]).reshape(3, 32, CH)
-            v = jnp.where(node_row[:, cols][None] == iota((3, 32, CH), 1), v, 0.0)
+            v = mm(field_s[...], colhot[:, cols])
+            v = jnp.concatenate([v[:96] + v[96:192], v[192:288] + v[288:]], axis=0)
+            v = v.reshape(6, 32, CH)
+            v = jnp.where(node_row[:, cols][None] == iota((1, 32, CH), 1), v, 0.0)
             v = jnp.sum(v, axis=1, keepdims=True)
-            v = jnp.concatenate([v, target_ref[:, cols].astype(F32)[None]], axis=0)
-            slots = slot_s[:, cols].astype(jnp.int32)[None] == iota((4, CAP, CH), 1)
-            v = jnp.where(slots, v, 0.0).reshape(4 * CAP, CH)
+            name = target_ref[:, cols].astype(F32)[None]
+            v = jnp.concatenate([v[:3], name, v[3:]], axis=0)
+            slots = slot_s[:, cols].astype(jnp.int32)[None] == iota((1, CAP, CH), 1)
+            v = jnp.where(slots, v, 0.0).reshape(7 * CAP, CH)
+            v = jnp.concatenate([v, jnp.zeros((CAP, CH), F32)], axis=0)
             for p in pieces(v, 2):
                 acc = acc + mm_nt(desthot[:, cols], p)
-        abuf[t] = acc.reshape(D // 8, 8, 128)
-
-    def a2a_1(t):
-        copies = []
-        for o, (dg, dx) in enumerate(gx_partners):
-            to_g, to_s = at_gx(dg, dx)
-            copies.append(
-                pltpu.make_async_remote_copy(
-                    src_ref=abuf.at[t, to_g * X + to_s // W],
-                    dst_ref=r1.at[t, pl.ds(8 * (o + 1), 8)],
-                    send_sem=a1_send.at[t, o],
-                    recv_sem=a1_recv.at[t, o],
-                    device_id=(to_g, to_s),
-                    device_id_type=MESH,
-                )
-            )
-            copies[-1].start()
-        r1[t, 0:8] = abuf[t, g * X + x]
-        return copies
-
-    def a2a_2(t, first):
-        for c in first:
-            c.wait_recv()
-        for d in range(W):
-            r1t[t, d] = r1[t, pl.ds(d, D // W, stride=W), :]
-        copies = []
-        for dw in range(1, W):
-            to = at_w(dw)
-            copies.append(
-                pltpu.make_async_remote_copy(
-                    src_ref=r1t.at[t, lax.rem(w + dw, W)],
-                    dst_ref=r3.at[t, dw],
-                    send_sem=a2_send.at[t, dw - 1],
-                    recv_sem=a2_recv.at[t, dw - 1],
-                    device_id=to,
-                    device_id_type=MESH,
-                )
-            )
-            copies[-1].start()
-        r3[t, 0] = r1t[t, w]
-        return copies
-
-    def place(t, second):
-        for c in second:
-            c.wait_recv()
-        got = r3[t].reshape(D, 128).T
-        name = got[96:128]
+        abuf[:, 0, :] = acc[:, 0:128]
+        abuf[:, 1, :] = acc[:, 128:256]
+
+    def all_to_all():
+        for n, (to_g, to_s) in enumerate(others):
+            pltpu.make_async_remote_copy(
+                src_ref=abuf.at[to_g * S + to_s],
+                dst_ref=arrived.at[n + 1],
+                send_sem=all_send,
+                recv_sem=all_recv,
+                device_id=(to_g, to_s),
+                device_id_type=MESH,
+            ).start()
+        arrived[0] = abuf[g * S + s]
+        return pltpu.make_async_remote_copy(
+            src_ref=abuf.at[0 : D - 1],
+            dst_ref=arrived.at[1:D],
+            send_sem=all_send,
+            recv_sem=all_recv,
+            device_id=others[0],
+            device_id_type=MESH,
+        )
+
+    def place():
+        got = [arrived[:, t, :].T for t in range(ITERS)]
+        name = got[0][96:128]
         high = jnp.floor(name * (1.0 / 128.0))
         low = name - 128.0 * high
-        acc = jnp.zeros((96, 128), F32)
+        upper = [v.astype(BF16).astype(F32) for v in got]
+        lower = [v - u for v, u in zip(got, upper)]
+        acc = jnp.zeros((192, 128), F32)
         for q in range(CAP // 4):
             left, right = [], []
             for z in range(4 * q, 4 * q + 4):
                 right.append(onehot(low[z : z + 1] == iota((128, D), 0).astype(F32)))
                 hit = high[z : z + 1] == iota((16, D), 0).astype(F32)
-                v = jnp.concatenate(
-                    [jnp.where(hit, got[32 * k + z : 32 * k + z + 1], 0.0) for k in range(3)], axis=0
-                )
-                left.append(jnp.concatenate(pieces(v, 2), axis=0))
+                v = [
+                    jnp.where(hit, part[t][32 * k + z : 32 * k + z + 1], 0.0)
+                    for part in (upper, lower)
+                    for t in range(ITERS)
+                    for k in range(3)
+                ]
+                left.append(jnp.concatenate(v, axis=0).astype(BF16))
             acc = acc + mm_nt(jnp.concatenate(left, axis=1), jnp.concatenate(right, axis=1))
-        acc = acc[:48] + acc[48:]
-        for k in range(3):
-            for h in range(16):
-                load_ref[t, k : k + 1, 128 * h : 128 * h + 128] = acc[16 * k + h : 16 * k + h + 1]
+        acc = acc[:96] + acc[96:]
+        for t in range(ITERS):
+            for k in range(3):
+                for h in range(16):
+                    n = (3 * t + k) * 16 + h
+                    load_ref[k, t : t + 1, 128 * h : 128 * h + 128] = acc[n : n + 1]
 
     def write_adjoint():
         own = state[UP : UP + ROWS].reshape(ROWS * 8, LANES)
@@ -518,31 +522,38 @@
 
     setup_rows()
     sides_finish()
-    row_late = row_copies(10, slice(384, 512))
+    fill_rows()
+    row_late = (
+        state_rows(10, last_tile)
+        + state_rows(12, slice(0, 128))
+        + oi_rows(14, last_tile)
+        + scale_rows(16, last_tile)
+    )
     for c in row_late:
         c.start()
-    fill_rows(UP, ROWS - DOWN - 1)
+    sweep_0_inner()
     for c in row_early + row_late:
         c.wait_recv()
-    for c in row_late + row_early:
+    sweep_0_outer()
+    for c in side_copies + row_early + row_late:
         c.wait_send()
-    fill_rows(-UP, UP)
-    fill_rows(ROWS - DOWN - 1, ROWS + DOWN)
-    sweep(0)
     sweep(1)
-    gather(0)
-    first_0 = a2a_1(0)
+    tractions(0)
     sweep(2)
     sweep(3)
-    gather(1)
-    first_1 = a2a_1(1)
-    second_0 = a2a_2(0, first_0)
+    tractions(1)
+    gather()
+    exchange = all_to_all()
     write_adjoint()
-    second_1 = a2a_2(1, first_1)
-    place(0, second_0)
-    place(1, second_1)
-    for c in side_copies + first_0 + first_1 + second_0 + second_1:
-        c.wait_send()
+    out_copy = pltpu.make_async_copy(out_ref, out_hbm, out_sem.at[0])
+    out_copy.start()
+    exchange.wait_recv()
+    place()
+    load_copy = pltpu.make_async_copy(load_ref, load_hbm, out_sem.at[1])
+    load_copy.start()
+    exchange.wait_send()
+    out_copy.wait()
+    load_copy.wait()
 
 
 def on_device(
@@ -560,12 +571,14 @@
     iface_target,
     iface_count,
 ):
-    vmem = pl.BlockSpec(memory_space=pltpu.VMEM)
+    hbm = pl.BlockSpec(memory_space=pl.ANY)
     D = G * S
-    XG = D // W
     dma = pltpu.SemaphoreType.DMA
     I32 = jnp.int32
     scratch = [
+        pltpu.VMEM((COMP, ROWS, COLS), F32),
+        pltpu.VMEM((3, ITERS, IF_CAP), F32),
+        dma((2,)),
         pltpu.VMEM((COMP, ROWS, COLS), F32),
         pltpu.VMEM((COMP, ROWS, COLS), F32),
         pltpu.VMEM((ROWS, COLS), F32),
@@ -579,6 +592,8 @@
         pltpu.VMEM((1, 1), I32),
         dma((11,)),
         pltpu.VMEM((UP + ROWS + DOWN, 8, LANES), F32),
+        pltpu.VMEM((UP + ROWS + DOWN, 8, LANES), F32),
+        pltpu.VMEM((ITERS * 192, LANES), BF16),
         pltpu.VMEM((O_UP + ROWS + O_DOWN, 8, LANES), F32),
         pltpu.VMEM((O_UP + ROWS + O_DOWN, 8, LANES), F32),
         pltpu.VMEM((4, 16, LANES), F32),
@@ -594,31 +609,27 @@
         pltpu.VMEM((2, ROWS, 8, 128), F32),
         pltpu.VMEM((2, 4, 16, 128), F32),
         pltpu.VMEM((2, 4, 16, 128), F32),
-        pltpu.VMEM((ITERS, XG, 8, 128), F32),
-        pltpu.VMEM((ITERS, D, 128), F32),
-        pltpu.VMEM((ITERS, W, XG, 128), F32),
-        pltpu.VMEM((ITERS, W, XG, 128), F32),
-        dma((16,)),
-        dma((16,)),
-        dma((ITERS, XG - 1)),
-        dma((ITERS, XG - 1)),
-        dma((ITERS, W - 1)),
-        dma((ITERS, W - 1)),
+        pltpu.VMEM((D, ITERS, 128), F32),
+        pltpu.VMEM((D, ITERS, 128), F32),
+        dma((18,)),
+        dma((18,)),
+        dma,
+        dma,
     ]
     call = pl.pallas_call(
         functools.partial(kernel, G, S),
         out_shape=(
             jax.ShapeDtypeStruct((COMP, ROWS, COLS), F32),
-            jax.ShapeDtypeStruct((ITERS, 3, IF_CAP), F32),
+            jax.ShapeDtypeStruct((3, ITERS, IF_CAP), F32),
         ),
-        in_specs=[pl.BlockSpec(memory_space=pl.ANY)] * 11,
-        out_specs=(vmem, vmem),
+        in_specs=[hbm] * 11,
+        out_specs=(hbm, hbm),
         scratch_shapes=scratch,
         compiler_params=pltpu.CompilerParams(
             collective_id=0, has_side_effects=True, vmem_limit_bytes=62 * 1024 * 1024
         ),
     )
-    return call(
+    adjoint, load = call(
         adjoint_start,
         objective_grad,
         diagonal,
@@ -631,6 +642,33 @@
         iface_target.reshape(1, IF_CAP),
         iface_count.reshape(1, 1),
     )
+    adjoint, load = hand_out(adjoint, load)
+    return adjoint, load.transpose(1, 0, 2)
+
+
+def hand_out_kernel(a, b, a_out, b_out, a_v, b_v, sem):
+    for start, end in (((a, b), (a_v, b_v)), ((a_v, b_v), (a_out, b_out))):
+        copies = [pltpu.make_async_copy(start[i], end[i], sem.at[i]) for i in range(2)]
+        for c in copies:
+            c.start()
+        for c in copies:
+            c.wait()
+
+
+def hand_out(a, b):
+    hbm = pl.BlockSpec(memory_space=pl.ANY)
+    return pl.pallas_call(
+        hand_out_kernel,
+        out_shape=(jax.ShapeDtypeStruct(a.shape, F32), jax.ShapeDtypeStruct(b.shape, F32)),
+        in_specs=[hbm, hbm],
+        out_specs=(hbm, hbm),
+        scratch_shapes=[
+            pltpu.VMEM(a.shape, F32),
+            pltpu.VMEM(b.shape, F32),
+            pltpu.SemaphoreType.DMA((2,)),
+        ],
+        compiler_params=pltpu.CompilerParams(vmem_limit_bytes=62 * 1024 * 1024),
+    )(a, b)
 
 
 def solution(mesh):

time: 40.7 us -> 37.1 us (0.912)
  local copies, waits for them, and re-layouts: 3.19 us -> 0 us
    pallas_call x1, Pallas kernels: 36 us -> 34 us  [on_device(): call(adjoint_start, objective_grad, diagonal, connect, element_scale, ele...]
    pallas_call x0 -> x1, Pallas kernels: none -> 1.7 us  [hand_out(): pl.pallas_call(hand_out_kernel, out_shape=(jax.ShapeDtypeStruct(a.shape,...]
    unnamed x1 -> x0, local copies, waits for them, and re-layouts: 1.69 us -> none
    pallas_call x1 -> x0, local copies, waits for them, and re-layouts: 1.5 us -> none  [on_device(): call(adjoint_start, objective_grad, diagonal, connect, element_scale, ele...]
where the time goes in v4:
time: 37.1 us; the launch traced here: 37 us
  Pallas kernels  35.7 us (96%)
  between operations  1.29 us (3%)
    pallas_call x1, Pallas kernels, on_device(): call(adjoint_start, objective_grad, diagonal, connect, element_scale, ele...  34 us
    pallas_call x1, Pallas kernels, hand_out(): pl.pallas_call(hand_out_kernel, out_shape=(jax.ShapeDtypeStruct(a.shape,...  1.7 us

profile of v4, /device:TPU:1, one launch (start us, length us, event | category | flops | bytes accessed | tf_op | source)
XLA Modules:
  0.0 37.0 jit_solution(15686484859913977881)
XLA Ops:
  1.3 34.0 %shard_map.122 = (f32[6,32,384]{2,1,0:T(8,128)}, f32[3,2,2048]{2,1,0:T(2,128)}) custom-call(f32[6,32,384]{2,1,0:T(8,128)} %adj_hbm.1, f32[6,32,384]{2,1,0:T(8,128)} %obj_hbm.1, f32[32,384]{1,0:T(8,128)} %diag_hbm.1, s32[64,338]{1,0:T(8,128)} %conn_hbm.1, f32[64,338]{1,0:T(8,128)} %scale_hbm.1, bf16[64,64]{1,0:T(8,128)(2,1)} %em_hbm.1, f32[3,6]{1,0:T(4,128)} %tm_hbm.1, ...), custom_call_target="tpu_custom_call" | custom-call | tf_op jit(solution)/shard_map/pallas_call | solution.py:632
  35.3 1.7 %shard_map.123 = (f32[6,32,384]{2,1,0:T(8,128)}, f32[3,2,2048]{2,1,0:T(2,128)}) custom-call(f32[6,32,384]{2,1,0:T(8,128)} %get-tuple-element.6.a, f32[3,2,2048]{2,1,0:T(2,128)} %get-tuple-element.7.b), custom_call_target="tpu_custom_call" | custom-call | tf_op jit(solution)/shard_map/pallas_call | solution.py:660

commit v5 on v4

--- a/solution.py
+++ b/solution.py
@@ -13,7 +13,7 @@
 IF_CAP = 2048
 CAP = 32
 ITERS = 2
-SWEEPS = 2
+W = 8
 LANES = 512
 UP, DOWN = 11, 10
 O_UP, O_DOWN = 8, 7
@@ -130,6 +130,10 @@
     colhot,
     desthot,
     slot_s,
+    names,
+    tile_0,
+    know_x,
+    know_y,
     side_send,
     side_recv,
     sscale_send,
@@ -171,8 +175,30 @@
     for c in loads:
         c.start()
     barrier = pltpu.get_barrier_semaphore()
-    others = [at(dg, ds) for ds in range(S) for dg in range(G)][1:]
-    for t in others:
+    X, Z = S // W, W // 2
+    x, z, core = s // W, lax.rem(s, W) // 2, lax.rem(s, 2)
+
+    def hops(offset):
+        dg, dx, dz, dc = offset
+        steps = [min(dg, G - dg), min(dx, X - dx), min(dz, Z - dz)]
+        return (sum(n > 0 for n in steps), sum(steps), dc)
+
+    offsets = [
+        (dg, dx, dz, dc) for dz in range(Z) for dx in range(X) for dg in range(G) for dc in range(2)
+    ]
+    others = [
+        (
+            lax.rem(g + dg, G),
+            (lax.rem(x + dx, X) * Z + lax.rem(z + dz, Z)) * 2 + lax.rem(core + dc, 2),
+        )
+        for dg, dx, dz, dc in sorted(offsets[1:], key=hops, reverse=True)
+    ]
+    here = s % W
+    line_w = [(g, s - here + lax.rem(here + n, W)) for n in range(1, W)]
+    line_x = [at(0, W * n) for n in range(1, S // W)]
+    line_y = [at(n, 0) for n in range(1, G)]
+    near = line_y + [at(0, -1), at(0, 1)] + line_w + line_x
+    for t in near:
         pl.semaphore_signal(barrier, inc=1, device_id=t, device_id_type=MESH)
 
     lane = iota((COLS, LANES), 1)
@@ -243,6 +269,33 @@
             remote(n, scale_own.at[:, 8:16, cols], scale_up.at[:, :, cols], at(1, 0)),
             remote(n + 1, scale_own.at[:, 0:8, cols], scale_down.at[:, :, cols], at(-1, 0)),
         ]
+
+    pl.semaphore_wait(barrier, len(near))
+    edges = (slice(0, DOWN), slice(ROWS - UP, ROWS))
+    middle = slice(DOWN, ROWS - UP)
+    sides = (at(0, -1), at(0, 1))
+
+    def side_rows(n, rows):
+        return [
+            remote(n + k, side_send.at[k, rows], side_recv.at[k, rows], sides[k]) for k in range(2)
+        ]
+
+    side_edges = side_rows(0, edges[0]) + side_rows(2, edges[1])
+    side_edges += [remote(4 + k, sscale_send.at[k], sscale_recv.at[k], sides[k]) for k in range(2)]
+    side_middle = side_rows(6, middle)
+    tile_0[0:UP] = state[ROWS : UP + ROWS, :, 0:128]
+    tile_0[UP:] = state[UP : UP + DOWN, :, 0:128]
+    early, last_tile = slice(0, 384), slice(384, 512)
+    row_early = state_rows(8, slice(128, 384)) + oi_rows(10, early) + scale_rows(12, early)
+    row_early += [
+        remote(14, tile_0.at[0:UP], state.at[0:UP, :, 0:128], at(1, 0)),
+        remote(15, tile_0.at[UP:], state.at[UP + ROWS :, :, 0:128], at(-1, 0)),
+    ]
+    scale_early = side_edges[4:] + row_early[4:6]
+    for c in side_edges[:4] + row_early[:4] + row_early[6:] + side_middle:
+        c.start()
+    for t in line_x:
+        pl.semaphore_signal(know_x, inc=1, device_id=t, device_id_type=MESH)
 
     loads[3].wait()
     loads[4].wait()
@@ -272,16 +325,7 @@
     for a in range(4):
         sscale_send[0, a] = turn(scale_own[a, :, 0:128], 32)
         sscale_send[1, a] = pack_right(scale_own[a, :, 256:384], scale_own[a, :, 384:512], 80)
-    pl.semaphore_wait(barrier, len(others))
-    side_copies = [
-        remote(0, side_send.at[0], side_recv.at[0], at(0, -1)),
-        remote(1, side_send.at[1], side_recv.at[1], at(0, 1)),
-        remote(2, sscale_send.at[0], sscale_recv.at[0], at(0, -1)),
-        remote(3, sscale_send.at[1], sscale_recv.at[1], at(0, 1)),
-    ]
-    early, last_tile = slice(0, 384), slice(384, 512)
-    row_early = state_rows(4, slice(128, 384)) + oi_rows(6, early) + scale_rows(8, early)
-    for c in side_copies + row_early:
+    for c in scale_early:
         c.start()
 
     loads[5].wait()
@@ -292,21 +336,22 @@
     wide = mm_nt(left, e_hot)
     wmat[...] = jnp.where(((rr >> 4) & 7) == ((cc >> 4) & 7), wide, 0.0).astype(BF16)
 
-    def sides_finish():
-        for c in side_copies:
-            c.wait_recv()
-        for p in range(0, ROWS, 8):
-            lane = iota((8, 8, 128), 2)
-            right, left = side_recv[0, p : p + 8], side_recv[1, p : p + 8]
-            own = state[UP + p : UP + p + 8, :, 384:512]
-            state[UP + p : UP + p + 8, :, 384:512] = jnp.where(
-                lane < 32, own, jnp.where(lane < 80, right, left)
-            )
-            own = oi[O_UP + p : O_UP + p + 8, :, 384:512]
-            both = jnp.where(lane < 80, left, right)
-            oi[O_UP + p : O_UP + p + 8, :, 384:512] = jnp.where(
-                lane < 32, own, jnp.where(lane < 80, turn(both, -48), turn(both, 48))
-            )
+    def sides_merge(rows):
+        lo, hi = rows.start, rows.stop
+        lane = iota((hi - lo, 8, 128), 2)
+        right, left = side_recv[0, rows], side_recv[1, rows]
+        st, ob = slice(UP + lo, UP + hi), slice(O_UP + lo, O_UP + hi)
+        own = state[st, :, 384:512]
+        own = jnp.where(lane < 32, own, jnp.where(lane < 80, right, left))
+        state[st, :, 0:128], state[st, :, 384:512] = fill(state[st, :, 0:128], own)
+        both = jnp.where(lane < 80, left, right)
+        oi[ob, :, 384:512] = jnp.where(
+            lane < 32,
+            oi[ob, :, 384:512],
+            jnp.where(lane < 80, turn(both, -48), turn(both, 48)),
+        )
+
+    def sides_merge_scale():
         lane = iota((16, 128), 1)
         for a in range(4):
             scale_own[a, :, 384:512] = jnp.where(
@@ -324,11 +369,10 @@
         three_new = jnp.where(lane >= 125, turn(first, -6), three_new)
         return first_new, three_new
 
-    def fill_rows():
-        for r in range(UP, UP + ROWS, 8):
-            state[r : r + 8, :, 0:128], state[r : r + 8, :, 384:512] = fill(
-                state[r : r + 8, :, 0:128], state[r : r + 8, :, 384:512]
-            )
+    def fill_arrived(lo, hi):
+        v = state[lo:hi, :, 0:128]
+        lane = iota(v.shape, 2)
+        state[lo:hi, :, 0:128] = jnp.where(lane < 3, turn(state[lo:hi, :, 384:512], 6), v)
 
     def scale_row(a, e, cols):
         if e < 5:
@@ -425,9 +469,15 @@
             before = mm(hot.astype(BF16), tri) + carry
             slot_s[:, cols] = jnp.sum(before * hot, axis=0, keepdims=True)
             carry = carry + jnp.sum(hot, axis=1, keepdims=True)
+        name = jnp.zeros((D, 128), F32)
         for b in range(IF_CAP // CH):
             cols = slice(CH * b, CH * b + CH)
             colhot[:, cols] = onehot(e_lane[:, cols] == iota((LANES, CH), 0))
+            slots = slot_s[:, cols].astype(jnp.int32) + 96 == iota((128, CH), 0)
+            for p in pieces(target_ref[:, cols].astype(F32), 2):
+                p = jnp.where(slots, p.astype(F32), 0.0).astype(BF16)
+                name = name + mm_nt(desthot[:, cols], p)
+        names[...] = name
 
     def tractions(t):
         lane = iota((1, 256), 1)
@@ -452,14 +502,13 @@
             v = v.reshape(6, 32, CH)
             v = jnp.where(node_row[:, cols][None] == iota((1, 32, CH), 1), v, 0.0)
             v = jnp.sum(v, axis=1, keepdims=True)
-            name = target_ref[:, cols].astype(F32)[None]
-            v = jnp.concatenate([v[:3], name, v[3:]], axis=0)
             slots = slot_s[:, cols].astype(jnp.int32)[None] == iota((1, CAP, CH), 1)
-            v = jnp.where(slots, v, 0.0).reshape(7 * CAP, CH)
-            v = jnp.concatenate([v, jnp.zeros((CAP, CH), F32)], axis=0)
+            none = jnp.zeros((CAP, CH), BF16)
             for p in pieces(v, 2):
+                p = jnp.where(slots, p.astype(F32), 0.0).astype(BF16).reshape(2, 3 * CAP, CH)
+                p = jnp.concatenate([p[0], none, p[1], none], axis=0)
                 acc = acc + mm_nt(desthot[:, cols], p)
-        abuf[:, 0, :] = acc[:, 0:128]
+        abuf[:, 0, :] = acc[:, 0:128] + names[...]
         abuf[:, 1, :] = acc[:, 128:256]
 
     def all_to_all():
@@ -521,21 +570,27 @@
         out_ref[...] = pick_rows(unperm, pick(own, back)).reshape(COMP, ROWS, COLS)
 
     setup_rows()
-    sides_finish()
-    fill_rows()
-    row_late = (
-        state_rows(10, last_tile)
-        + state_rows(12, slice(0, 128))
-        + oi_rows(14, last_tile)
-        + scale_rows(16, last_tile)
-    )
+    for c in side_edges:
+        c.wait_recv()
+    for rows in edges:
+        sides_merge(rows)
+    sides_merge_scale()
+    row_late = state_rows(16, last_tile) + oi_rows(18, last_tile) + scale_rows(20, last_tile)
     for c in row_late:
         c.start()
+    pl.semaphore_wait(know_x, len(line_x))
+    for t in line_y:
+        pl.semaphore_signal(know_y, inc=1, device_id=t, device_id_type=MESH)
+    for c in side_middle:
+        c.wait_recv()
+    sides_merge(middle)
     sweep_0_inner()
     for c in row_early + row_late:
         c.wait_recv()
+    fill_arrived(0, UP)
+    fill_arrived(UP + ROWS, UP + ROWS + DOWN)
     sweep_0_outer()
-    for c in side_copies + row_early + row_late:
+    for c in side_edges + side_middle + row_early + row_late:
         c.wait_send()
     sweep(1)
     tractions(0)
@@ -543,6 +598,7 @@
     sweep(3)
     tractions(1)
     gather()
+    pl.semaphore_wait(know_y, len(line_y))
     exchange = all_to_all()
     write_adjoint()
     out_copy = pltpu.make_async_copy(out_ref, out_hbm, out_sem.at[0])
@@ -605,14 +661,18 @@
         pltpu.VMEM((LANES, IF_CAP), BF16),
         pltpu.VMEM((D, IF_CAP), BF16),
         pltpu.VMEM((1, IF_CAP), F32),
+        pltpu.VMEM((D, 128), F32),
+        pltpu.VMEM((UP + DOWN, 8, 128), F32),
+        pltpu.SemaphoreType.REGULAR,
+        pltpu.SemaphoreType.REGULAR,
         pltpu.VMEM((2, ROWS, 8, 128), F32),
         pltpu.VMEM((2, ROWS, 8, 128), F32),
         pltpu.VMEM((2, 4, 16, 128), F32),
         pltpu.VMEM((2, 4, 16, 128), F32),
         pltpu.VMEM((D, ITERS, 128), F32),
         pltpu.VMEM((D, ITERS, 128), F32),
-        dma((18,)),
-        dma((18,)),
+        dma((22,)),
+        dma((22,)),
         dma,
         dma,
     ]
@@ -647,12 +707,17 @@
 
 
 def hand_out_kernel(a, b, a_out, b_out, a_v, b_v, sem):
-    for start, end in (((a, b), (a_v, b_v)), ((a_v, b_v), (a_out, b_out))):
-        copies = [pltpu.make_async_copy(start[i], end[i], sem.at[i]) for i in range(2)]
-        for c in copies:
-            c.start()
-        for c in copies:
-            c.wait()
+    parts = [(a.at[c], a_v.at[c], a_out.at[c]) for c in range(COMP)] + [(b, b_v, b_out)]
+    parts = parts[-1:] + parts[:-1]
+    loads = [pltpu.make_async_copy(p[0], p[1], sem.at[0, n]) for n, p in enumerate(parts)]
+    stores = [pltpu.make_async_copy(p[1], p[2], sem.at[1, n]) for n, p in enumerate(parts)]
+    for c in loads:
+        c.start()
+    for load, store in zip(loads, stores):
+        load.wait()
+        store.start()
+    for c in stores:
+        c.wait()
 
 
 def hand_out(a, b):
@@ -665,7 +730,7 @@
         scratch_shapes=[
             pltpu.VMEM(a.shape, F32),
             pltpu.VMEM(b.shape, F32),
-            pltpu.SemaphoreType.DMA((2,)),
+            pltpu.SemaphoreType.DMA((2, COMP + 1)),
         ],
         compiler_params=pltpu.CompilerParams(vmem_limit_bytes=62 * 1024 * 1024),
     )(a, b)

time: 37.1 us -> 35.3 us (0.951)
  Pallas kernels: 35.7 us -> 33.8 us
    pallas_call x1, Pallas kernels: 34 us -> 32.2 us  [on_device(): call(adjoint_start, objective_grad, diagonal, connect, element_scale, ele...]
where the time goes in v5:
time: 35.3 us; the launch traced here: 35.1 us
  Pallas kernels  33.8 us (96%)
  between operations  1.29 us (4%)
    pallas_call x1, Pallas kernels, on_device(): call(adjoint_start, objective_grad, diagonal, connect, element_scale, ele...  32.2 us
    pallas_call x1, Pallas kernels, hand_out(): pl.pallas_call(hand_out_kernel, out_shape=(jax.ShapeDtypeStruct(a.shape,...  1.68 us

profile of v5, /device:TPU:1, one launch (start us, length us, event | category | flops | bytes accessed | tf_op | source)
XLA Modules:
  0.0 35.1 jit_solution(16601649967321169689)
XLA Ops:
  1.3 32.2 %shard_map.122 = (f32[6,32,384]{2,1,0:T(8,128)}, f32[3,2,2048]{2,1,0:T(2,128)}) custom-call(f32[6,32,384]{2,1,0:T(8,128)} %adj_hbm.1, f32[6,32,384]{2,1,0:T(8,128)} %obj_hbm.1, f32[32,384]{1,0:T(8,128)} %diag_hbm.1, s32[64,338]{1,0:T(8,128)} %conn_hbm.1, f32[64,338]{1,0:T(8,128)} %scale_hbm.1, bf16[64,64]{1,0:T(8,128)(2,1)} %em_hbm.1, f32[3,6]{1,0:T(4,128)} %tm_hbm.1, ...), custom_call_target="tpu_custom_call" | custom-call | tf_op jit(solution)/shard_map/pallas_call | solution.py:692
  33.4 1.7 %shard_map.123 = (f32[6,32,384]{2,1,0:T(8,128)}, f32[3,2,2048]{2,1,0:T(2,128)}) custom-call(f32[6,32,384]{2,1,0:T(8,128)} %get-tuple-element.6.a, f32[3,2,2048]{2,1,0:T(2,128)} %get-tuple-element.7.b), custom_call_target="tpu_custom_call" | custom-call | tf_op jit(solution)/shard_map/pallas_call | solution.py:725

commit v6 on v5

--- a/solution.py
+++ b/solution.py
@@ -100,9 +100,8 @@
     target_hbm,
     count_hbm,
     out_hbm,
-    load_hbm,
+    arrived,
     out_ref,
-    load_ref,
     out_sem,
     adj_ref,
     obj_ref,
@@ -130,6 +129,8 @@
     colhot,
     desthot,
     slot_s,
+    slothot,
+    rowhot,
     names,
     tile_0,
     know_x,
@@ -139,7 +140,6 @@
     sscale_send,
     sscale_recv,
     abuf,
-    arrived,
     halo_send,
     halo_recv,
     all_send,
@@ -215,8 +215,8 @@
     scaled_obj = (obj_ref[...] * inverse[None]).reshape(COMP * ROWS, COLS)
     m = iota((ROWS * 8, ROWS), 0)
     perm_inv = onehot(((m & 7) == COMP) & ((m >> 3) == iota((ROWS * 8, ROWS), 1)))
-    first = pick_rows(perm, scaled_obj) + pick_rows(perm_inv, inverse)
-    oi[O_UP : O_UP + ROWS] = pick(first, sel).reshape(ROWS, 8, LANES)
+    first = pick_rows(perm, scaled_obj, 2) + pick_rows(perm_inv, inverse, 2)
+    oi[O_UP : O_UP + ROWS] = pick(first, sel, 2).reshape(ROWS, 8, LANES)
 
     def remote(n, src, dst, dev):
         return pltpu.make_async_remote_copy(
@@ -329,12 +329,24 @@
         c.start()
 
     loads[5].wait()
-    r = iota((LANES, 64), 0)
-    e_hot = onehot((r >> 7) * 16 + (r & 15) == iota((LANES, 64), 1))
-    left = mm(e_hot, em_ref[...]).astype(BF16)
-    rr, cc = iota((LANES, LANES), 0), iota((LANES, LANES), 1)
-    wide = mm_nt(left, e_hot)
-    wmat[...] = jnp.where(((rr >> 4) & 7) == ((cc >> 4) & 7), wide, 0.0).astype(BF16)
+    r, n = iota((LANES, 64), 0), iota((LANES, 64), 1)
+    r_b, r_a = r & 15, (r >> 7) * 16
+    left = mm(onehot(r_a + r_b == n), em_ref[...]).astype(BF16)
+
+    def columns(mask):
+        return mm_nt(left, onehot(mask))
+
+    rr, cc = (iota((LANES, LANES), 0) >> 4) & 7, (iota((LANES, LANES), 1) >> 4) & 7
+    same = jnp.where(rr == cc, columns(r_a + r_b == n), 0.0)
+    after, before = rr == cc - 1, rr == cc + 1
+    one_after = jnp.where(after, columns((r_a + 15 == n) & (r_b == 0)), 0.0)
+    one_before = jnp.where(before, columns((r_a == n) & (r_b == 15)), 0.0)
+    two_after = jnp.where(after, columns((r_a + r_b + 14 == n) & (r_b < 2)), 0.0)
+    two_before = jnp.where(before, columns((r_a + r_b - 14 == n) & (r_b >= 14)), 0.0)
+    wmat[0] = (same + one_after + one_before).astype(BF16)
+    first, second = (cc == 0) | (cc == 6), (cc == 1) | (cc == 7)
+    shared = jnp.where(second, two_after, one_after) + jnp.where(first, two_before, one_before)
+    wmat[1] = (same + shared).astype(BF16)
 
     def sides_merge(rows):
         lo, hi = rows.start, rows.stop
@@ -391,7 +403,7 @@
             for a in range(4):
                 v = [src[UP + STARTS[e] + a, :, cols] * scale_row(a, e, cols) for e in elems]
                 parts.append(jnp.concatenate(v, axis=0).astype(BF16))
-            o = mm(jnp.concatenate(parts, axis=1), wmat[...])
+            o = mm(jnp.concatenate(parts, axis=1), wmat[q // 3])
             for row in rows:
                 terms = [
                     o[8 * n : 8 * n + 8, 128 * a : 128 * a + 128]
@@ -409,20 +421,17 @@
         for r0 in range(first, last, step):
             n = min(step, last - r0)
             lane = iota((n, 8, 128), 2)
-            low = lane & 15
             a0 = O_UP + r0
             tiles = [asm[a0 : a0 + n, :, 128 * q : 128 * q + 128] for q in range(4)]
             ahead = [turn(v, 1) for v in tiles]
             back = [turn(v, -1) for v in tiles]
             new = []
             for q in range(4):
-                before = jnp.where(lane == 0, ahead[(q + 3) % 4], ahead[q])
-                after = jnp.where(lane == 127, back[(q + 1) % 4], back[q])
-                more = jnp.where(low == 0, before, jnp.where(low == 15, after, 0.0))
-                if q == 3:
-                    pair = jnp.where(lane >= 96, lane - 96, lane)
-                    more = jnp.where((pair == 14) | (pair == 15), turn(tiles[3], -2), more)
-                    more = jnp.where((pair == 16) | (pair == 17), turn(tiles[3], 2), more)
+                more = jnp.where(
+                    lane == 0,
+                    ahead[(q + 3) % 4],
+                    jnp.where(lane == 127, back[(q + 1) % 4], 0.0),
+                )
                 cols = slice(128 * q, 128 * q + 128)
                 rhs = oi[a0 : a0 + n, :, cols]
                 inv = jnp.broadcast_to(oi[a0 : a0 + n, COMP : COMP + 1, cols], (n, 8, 128))
@@ -474,6 +483,8 @@
             cols = slice(CH * b, CH * b + CH)
             colhot[:, cols] = onehot(e_lane[:, cols] == iota((LANES, CH), 0))
             slots = slot_s[:, cols].astype(jnp.int32) + 96 == iota((128, CH), 0)
+            slothot[:, cols] = onehot(slot_s[:, cols].astype(jnp.int32) == iota((CAP, CH), 0))
+            rowhot[:, cols] = jnp.where(node_row[:, cols] == iota((32, CH), 0), 1.0, 0.0)
             for p in pieces(target_ref[:, cols].astype(F32), 2):
                 p = jnp.where(slots, p.astype(F32), 0.0).astype(BF16)
                 name = name + mm_nt(desthot[:, cols], p)
@@ -499,13 +510,12 @@
             cols = slice(CH * b, CH * b + CH)
             v = mm(field_s[...], colhot[:, cols])
             v = jnp.concatenate([v[:96] + v[96:192], v[192:288] + v[288:]], axis=0)
-            v = v.reshape(6, 32, CH)
-            v = jnp.where(node_row[:, cols][None] == iota((1, 32, CH), 1), v, 0.0)
+            v = v.reshape(6, 32, CH) * rowhot[:, cols][None]
             v = jnp.sum(v, axis=1, keepdims=True)
-            slots = slot_s[:, cols].astype(jnp.int32)[None] == iota((1, CAP, CH), 1)
             none = jnp.zeros((CAP, CH), BF16)
             for p in pieces(v, 2):
-                p = jnp.where(slots, p.astype(F32), 0.0).astype(BF16).reshape(2, 3 * CAP, CH)
+                p = jnp.broadcast_to(p.astype(F32), (6, CAP, CH)).astype(BF16)
+                p = (p * slothot[:, cols][None]).reshape(2, 3 * CAP, CH)
                 p = jnp.concatenate([p[0], none, p[1], none], axis=0)
                 acc = acc + mm_nt(desthot[:, cols], p)
         abuf[:, 0, :] = acc[:, 0:128] + names[...]
@@ -521,8 +531,9 @@
                 device_id=(to_g, to_s),
                 device_id_type=MESH,
             ).start()
-        arrived[0] = abuf[g * S + s]
-        return pltpu.make_async_remote_copy(
+        own = pltpu.make_async_copy(abuf.at[g * S + s], arrived.at[0], out_sem.at[1])
+        own.start()
+        return own, pltpu.make_async_remote_copy(
             src_ref=abuf.at[0 : D - 1],
             dst_ref=arrived.at[1:D],
             send_sem=all_send,
@@ -530,34 +541,6 @@
             device_id=others[0],
             device_id_type=MESH,
         )
-
-    def place():
-        got = [arrived[:, t, :].T for t in range(ITERS)]
-        name = got[0][96:128]
-        high = jnp.floor(name * (1.0 / 128.0))
-        low = name - 128.0 * high
-        upper = [v.astype(BF16).astype(F32) for v in got]
-        lower = [v - u for v, u in zip(got, upper)]
-        acc = jnp.zeros((192, 128), F32)
-        for q in range(CAP // 4):
-            left, right = [], []
-            for z in range(4 * q, 4 * q + 4):
-                right.append(onehot(low[z : z + 1] == iota((128, D), 0).astype(F32)))
-                hit = high[z : z + 1] == iota((16, D), 0).astype(F32)
-                v = [
-                    jnp.where(hit, part[t][32 * k + z : 32 * k + z + 1], 0.0)
-                    for part in (upper, lower)
-                    for t in range(ITERS)
-                    for k in range(3)
-                ]
-                left.append(jnp.concatenate(v, axis=0).astype(BF16))
-            acc = acc + mm_nt(jnp.concatenate(left, axis=1), jnp.concatenate(right, axis=1))
-        acc = acc[:96] + acc[96:]
-        for t in range(ITERS):
-            for k in range(3):
-                for h in range(16):
-                    n = (3 * t + k) * 16 + h
-                    load_ref[k, t : t + 1, 128 * h : 128 * h + 128] = acc[n : n + 1]
 
     def write_adjoint():
         own = state[UP : UP + ROWS].reshape(ROWS * 8, LANES)
@@ -599,17 +582,14 @@
     tractions(1)
     gather()
     pl.semaphore_wait(know_y, len(line_y))
-    exchange = all_to_all()
+    own, exchange = all_to_all()
     write_adjoint()
     out_copy = pltpu.make_async_copy(out_ref, out_hbm, out_sem.at[0])
     out_copy.start()
     exchange.wait_recv()
-    place()
-    load_copy = pltpu.make_async_copy(load_ref, load_hbm, out_sem.at[1])
-    load_copy.start()
+    own.wait()
     exchange.wait_send()
     out_copy.wait()
-    load_copy.wait()
 
 
 def on_device(
@@ -633,7 +613,6 @@
     I32 = jnp.int32
     scratch = [
         pltpu.VMEM((COMP, ROWS, COLS), F32),
-        pltpu.VMEM((3, ITERS, IF_CAP), F32),
         dma((2,)),
         pltpu.VMEM((COMP, ROWS, COLS), F32),
         pltpu.VMEM((COMP, ROWS, COLS), F32),
@@ -655,12 +634,14 @@
         pltpu.VMEM((4, 16, LANES), F32),
         pltpu.VMEM((4, 8, LANES), F32),
         pltpu.VMEM((4, 8, LANES), F32),
-        pltpu.VMEM((LANES, LANES), BF16),
+        pltpu.VMEM((2, LANES, LANES), BF16),
         pltpu.VMEM((8, 384), I32),
         pltpu.VMEM((64, 384), F32),
         pltpu.VMEM((LANES, IF_CAP), BF16),
         pltpu.VMEM((D, IF_CAP), BF16),
         pltpu.VMEM((1, IF_CAP), F32),
+        pltpu.VMEM((CAP, IF_CAP), BF16),
+        pltpu.VMEM((32, IF_CAP), F32),
         pltpu.VMEM((D, 128), F32),
         pltpu.VMEM((UP + DOWN, 8, 128), F32),
         pltpu.SemaphoreType.REGULAR,
@@ -669,7 +650,6 @@
         pltpu.VMEM((2, ROWS, 8, 128), F32),
         pltpu.VMEM((2, 4, 16, 128), F32),
         pltpu.VMEM((2, 4, 16, 128), F32),
-        pltpu.VMEM((D, ITERS, 128), F32),
         pltpu.VMEM((D, ITERS, 128), F32),
         dma((22,)),
         dma((22,)),
@@ -680,7 +660,7 @@
         functools.partial(kernel, G, S),
         out_shape=(
             jax.ShapeDtypeStruct((COMP, ROWS, COLS), F32),
-            jax.ShapeDtypeStruct((3, ITERS, IF_CAP), F32),
+            jax.ShapeDtypeStruct((D, ITERS, 128), F32),
         ),
         in_specs=[hbm] * 11,
         out_specs=(hbm, hbm),
@@ -689,7 +669,7 @@
             collective_id=0, has_side_effects=True, vmem_limit_bytes=62 * 1024 * 1024
         ),
     )
-    adjoint, load = call(
+    adjoint, arrived = call(
         adjoint_start,
         objective_grad,
         diagonal,
@@ -702,38 +682,68 @@
         iface_target.reshape(1, IF_CAP),
         iface_count.reshape(1, 1),
     )
-    adjoint, load = hand_out(adjoint, load)
+    adjoint, load = finish(adjoint, arrived)
     return adjoint, load.transpose(1, 0, 2)
 
 
-def hand_out_kernel(a, b, a_out, b_out, a_v, b_v, sem):
-    parts = [(a.at[c], a_v.at[c], a_out.at[c]) for c in range(COMP)] + [(b, b_v, b_out)]
-    parts = parts[-1:] + parts[:-1]
-    loads = [pltpu.make_async_copy(p[0], p[1], sem.at[0, n]) for n, p in enumerate(parts)]
-    stores = [pltpu.make_async_copy(p[1], p[2], sem.at[1, n]) for n, p in enumerate(parts)]
-    for c in loads:
-        c.start()
-    for load, store in zip(loads, stores):
-        load.wait()
-        store.start()
-    for c in stores:
-        c.wait()
-
-
-def hand_out(a, b):
+def finish_kernel(adj, arr, adj_out, load_out, adj_v, arrived, load_ref, sem):
+    arr_load = pltpu.make_async_copy(arr, arrived, sem.at[0])
+    adj_load = pltpu.make_async_copy(adj, adj_v, sem.at[1])
+    adj_store = pltpu.make_async_copy(adj_v, adj_out, sem.at[2])
+    load_store = pltpu.make_async_copy(load_ref, load_out, sem.at[3])
+    arr_load.start()
+    adj_load.start()
+    count = arr.shape[0]
+    arr_load.wait()
+    got = [arrived[:, t, :].T for t in range(ITERS)]
+    name = got[0][96:128]
+    high = jnp.floor(name * (1.0 / 128.0))
+    low = name - 128.0 * high
+    upper = [v.astype(BF16).astype(F32) for v in got]
+    lower = [v - u for v, u in zip(got, upper)]
+    acc = jnp.zeros((192, 128), F32)
+    for q in range(CAP // 4):
+        left, right = [], []
+        for z in range(4 * q, 4 * q + 4):
+            right.append(onehot(low[z : z + 1] == iota((128, count), 0).astype(F32)))
+            hit = high[z : z + 1] == iota((16, count), 0).astype(F32)
+            v = [
+                jnp.where(hit, part[t][32 * k + z : 32 * k + z + 1], 0.0)
+                for part in (upper, lower)
+                for t in range(ITERS)
+                for k in range(3)
+            ]
+            left.append(jnp.concatenate(v, axis=0).astype(BF16))
+        acc = acc + mm_nt(jnp.concatenate(left, axis=1), jnp.concatenate(right, axis=1))
+    acc = acc[:96] + acc[96:]
+    for t in range(ITERS):
+        for k in range(3):
+            for h in range(16):
+                n = (3 * t + k) * 16 + h
+                load_ref[k, t : t + 1, 128 * h : 128 * h + 128] = acc[n : n + 1]
+    load_store.start()
+    adj_load.wait()
+    adj_store.start()
+    load_store.wait()
+    adj_store.wait()
+
+
+def finish(adjoint, arrived):
     hbm = pl.BlockSpec(memory_space=pl.ANY)
+    load = (3, ITERS, IF_CAP)
     return pl.pallas_call(
-        hand_out_kernel,
-        out_shape=(jax.ShapeDtypeStruct(a.shape, F32), jax.ShapeDtypeStruct(b.shape, F32)),
+        finish_kernel,
+        out_shape=(jax.ShapeDtypeStruct(adjoint.shape, F32), jax.ShapeDtypeStruct(load, F32)),
         in_specs=[hbm, hbm],
         out_specs=(hbm, hbm),
         scratch_shapes=[
-            pltpu.VMEM(a.shape, F32),
-            pltpu.VMEM(b.shape, F32),
-            pltpu.SemaphoreType.DMA((2, COMP + 1)),
+            pltpu.VMEM(adjoint.shape, F32),
+            pltpu.VMEM(arrived.shape, F32),
+            pltpu.VMEM(load, F32),
+            pltpu.SemaphoreType.DMA((4,)),
         ],
         compiler_params=pltpu.CompilerParams(vmem_limit_bytes=62 * 1024 * 1024),
-    )(a, b)
+    )(adjoint, arrived)
 
 
 def solution(mesh):

time: 35.3 us -> 33.5 us (0.949)
  Pallas kernels: 33.8 us -> 32.1 us
    pallas_call x1, Pallas kernels: 32.2 us -> 29.7 us  [on_device(): call(adjoint_start, objective_grad, diagonal, connect, element_scale, ele...]
    pallas_call x1, Pallas kernels: 1.68 us -> 2.36 us  [finish(): pl.pallas_call(finish_kernel, out_shape=(jax.ShapeDtypeStruct(adjoint.sha...]
where the time goes in v6:
time: 33.5 us; the launch traced here: 33.4 us
  Pallas kernels  32.1 us (96%)
  between operations  1.29 us (4%)
    pallas_call x1, Pallas kernels, on_device(): call(adjoint_start, objective_grad, diagonal, connect, element_scale, ele...  29.7 us
    pallas_call x1, Pallas kernels, finish(): pl.pallas_call(finish_kernel, out_shape=(jax.ShapeDtypeStruct(adjoint.sha...  2.36 us

profile of v6, /device:TPU:1, one launch (start us, length us, event | category | flops | bytes accessed | tf_op | source)
XLA Modules:
  0.0 33.4 jit_solution(1498526743138342395)
XLA Ops:
  1.3 29.7 %shard_map.122 = (f32[6,32,384]{2,1,0:T(8,128)}, f32[128,2,128]{2,1,0:T(2,128)}) custom-call(f32[6,32,384]{2,1,0:T(8,128)} %adj_hbm.1, f32[6,32,384]{2,1,0:T(8,128)} %obj_hbm.1, f32[32,384]{1,0:T(8,128)} %diag_hbm.1, s32[64,338]{1,0:T(8,128)} %conn_hbm.1, f32[64,338]{1,0:T(8,128)} %scale_hbm.1, bf16[64,64]{1,0:T(8,128)(2,1)} %em_hbm.1, f32[3,6]{1,0:T(4,128)} %tm_hbm.1, ...), custom_call_target="tpu_custom_call" | custom-call | tf_op jit(solution)/shard_map/pallas_call | solution.py:672
  31.0 2.4 %shard_map.123 = (f32[6,32,384]{2,1,0:T(8,128)}, f32[3,2,2048]{2,1,0:T(2,128)}) custom-call(f32[6,32,384]{2,1,0:T(8,128)} %get-tuple-element.6.adj, f32[128,2,128]{2,1,0:T(2,128)} %get-tuple-element.7.arr), custom_call_target="tpu_custom_call" | custom-call | tf_op jit(solution)/shard_map/pallas_call | solution.py:734

commit v7 on v6

--- a/solution.py
+++ b/solution.py
@@ -115,8 +115,11 @@
     target_ref,
     count_ref,
     in_sem,
-    state_a,
-    state_b,
+    state,
+    state_1,
+    state_2,
+    state_3,
+    state_4,
     field_s,
     oi,
     asm,
@@ -146,8 +149,7 @@
     all_recv,
 ):
     D = G * S
-    states = (state_a, state_b)
-    state = state_a
+    states = (state, state_1, state_2, state_3, state_4)
     g = lax.axis_index("group")
     s = lax.axis_index("sub")
 
@@ -292,7 +294,7 @@
         remote(15, tile_0.at[UP:], state.at[UP + ROWS :, :, 0:128], at(-1, 0)),
     ]
     scale_early = side_edges[4:] + row_early[4:6]
-    for c in side_edges[:4] + row_early[:4] + row_early[6:] + side_middle:
+    for c in side_edges[:4] + row_early[:4] + row_early[6:]:
         c.start()
     for t in line_x:
         pl.semaphore_signal(know_x, inc=1, device_id=t, device_id_type=MESH)
@@ -325,7 +327,7 @@
     for a in range(4):
         sscale_send[0, a] = turn(scale_own[a, :, 0:128], 32)
         sscale_send[1, a] = pack_right(scale_own[a, :, 256:384], scale_own[a, :, 384:512], 80)
-    for c in scale_early:
+    for c in scale_early + side_middle:
         c.start()
 
     loads[5].wait()
@@ -396,7 +398,7 @@
         return jnp.broadcast_to(v, (8, 128))
 
     def products(t, elems, rows, begun=()):
-        src = states[t % 2]
+        src = states[t]
         for q in range(4):
             cols = slice(128 * q, 128 * q + 128)
             parts = []
@@ -412,17 +414,17 @@
                     if STARTS[e] + a == row and block_of(e) == owner(row)
                 ]
                 if row in begun:
-                    terms.append(asm[O_UP + row, :, cols])
-                asm[O_UP + row, :, cols] = total(terms)
+                    terms.append(asm[t, O_UP + row, :, cols])
+                asm[t, O_UP + row, :, cols] = total(terms)
 
     def update(t, first, last):
-        dst = states[(t + 1) % 2]
+        dst = states[t + 1]
         step = 4
         for r0 in range(first, last, step):
             n = min(step, last - r0)
             lane = iota((n, 8, 128), 2)
             a0 = O_UP + r0
-            tiles = [asm[a0 : a0 + n, :, 128 * q : 128 * q + 128] for q in range(4)]
+            tiles = [asm[t, a0 : a0 + n, :, 128 * q : 128 * q + 128] for q in range(4)]
             ahead = [turn(v, 1) for v in tiles]
             back = [turn(v, -1) for v in tiles]
             new = []
@@ -441,22 +443,19 @@
             for q in range(4):
                 dst[UP + r0 : UP + r0 + n, :, 128 * q : 128 * q + 128] = new[q]
 
-    def sweep(t):
-        products(t, range(*ACTIVE[t]), range(*UPDATED[t]))
-        update(t, *UPDATED[t])
-
-    INNER = range(6, 16)
-
-    def sweep_0_inner():
-        products(0, INNER, range(0, 31))
-        update(0, 1, 30)
-
-    def sweep_0_outer():
-        rows = [r for r in range(*UPDATED[0]) if r < 1 or r > 29]
-        products(0, [e for e in range(*ACTIVE[0]) if e not in INNER], rows, (0, 30))
-        update(0, UPDATED[0][0], 1)
-        update(0, 30, UPDATED[0][1])
-
+    def inner(t):
+        return range(6 + t, 16 - t)
+
+    def sweep_inner(t):
+        products(t, inner(t), range(3 * t, 31 - 3 * t))
+        update(t, 3 * t + 1, 30 - 3 * t)
+
+    def sweep_outer(t):
+        lo, hi = 3 * t + 1, 30 - 3 * t
+        rows = [r for r in range(*UPDATED[t]) if r < lo or r >= hi]
+        products(t, [e for e in range(*ACTIVE[t]) if e not in inner(t)], rows, (lo - 1, hi))
+        update(t, UPDATED[t][0], lo)
+        update(t, hi, UPDATED[t][1])
 
     CH = 512
     for c in loads[6:]:
@@ -499,7 +498,7 @@
                 row = jnp.where((lane & 7) == c, tm_ref[k : k + 1, c : c + 1], row)
             trac.append(jnp.where((iota((32, 256), 1) >> 3) == iota((32, 256), 0), row, 0.0))
         high, low = pieces(jnp.concatenate(trac, axis=0), 2)
-        own = state[UP : UP + ROWS].reshape(ROWS * 8, LANES)
+        own = states[2 * t + 2][UP : UP + ROWS].reshape(ROWS * 8, LANES)
         own_high, own_low = pieces(own, 2)
         field = mm(high, own_high) + (mm(high, own_low) + mm(low, own_high))
         field_s[192 * t : 192 * t + 192] = jnp.concatenate(pieces(field, 2), axis=0)
@@ -522,6 +521,8 @@
         abuf[:, 1, :] = acc[:, 128:256]
 
     def all_to_all():
+        own = pltpu.make_async_copy(abuf.at[g * S + s], arrived.at[0], out_sem.at[1])
+        own.start()
         for n, (to_g, to_s) in enumerate(others):
             pltpu.make_async_remote_copy(
                 src_ref=abuf.at[to_g * S + to_s],
@@ -531,9 +532,8 @@
                 device_id=(to_g, to_s),
                 device_id_type=MESH,
             ).start()
-        own = pltpu.make_async_copy(abuf.at[g * S + s], arrived.at[0], out_sem.at[1])
-        own.start()
-        return own, pltpu.make_async_remote_copy(
+        own.wait()
+        return pltpu.make_async_remote_copy(
             src_ref=abuf.at[0 : D - 1],
             dst_ref=arrived.at[1:D],
             send_sem=all_send,
@@ -543,7 +543,7 @@
         )
 
     def write_adjoint():
-        own = state[UP : UP + ROWS].reshape(ROWS * 8, LANES)
+        own = states[4][UP : UP + ROWS].reshape(ROWS * 8, LANES)
         lane = iota((LANES, COLS), 0)
         j, b = lane >> 4, lane & 15
         keep = ((j < 25) & (b < 15)) | ((j == 25) & (b > 0))
@@ -567,27 +567,27 @@
     for c in side_middle:
         c.wait_recv()
     sides_merge(middle)
-    sweep_0_inner()
+    for t in range(4):
+        sweep_inner(t)
     for c in row_early + row_late:
         c.wait_recv()
     fill_arrived(0, UP)
     fill_arrived(UP + ROWS, UP + ROWS + DOWN)
-    sweep_0_outer()
-    for c in side_edges + side_middle + row_early + row_late:
-        c.wait_send()
-    sweep(1)
+    sweep_outer(0)
+    sweep_outer(1)
     tractions(0)
-    sweep(2)
-    sweep(3)
+    sweep_outer(2)
+    sweep_outer(3)
     tractions(1)
     gather()
     pl.semaphore_wait(know_y, len(line_y))
-    own, exchange = all_to_all()
+    exchange = all_to_all()
     write_adjoint()
     out_copy = pltpu.make_async_copy(out_ref, out_hbm, out_sem.at[0])
     out_copy.start()
     exchange.wait_recv()
-    own.wait()
+    for c in side_edges + side_middle + row_early + row_late:
+        c.wait_send()
     exchange.wait_send()
     out_copy.wait()
 
@@ -626,11 +626,10 @@
         pltpu.VMEM((1, IF_CAP), I32),
         pltpu.VMEM((1, 1), I32),
         dma((11,)),
-        pltpu.VMEM((UP + ROWS + DOWN, 8, LANES), F32),
-        pltpu.VMEM((UP + ROWS + DOWN, 8, LANES), F32),
+        *[pltpu.VMEM((UP + ROWS + DOWN, 8, LANES), F32)] * 5,
         pltpu.VMEM((ITERS * 192, LANES), BF16),
         pltpu.VMEM((O_UP + ROWS + O_DOWN, 8, LANES), F32),
-        pltpu.VMEM((O_UP + ROWS + O_DOWN, 8, LANES), F32),
+        pltpu.VMEM((4, O_UP + ROWS + O_DOWN, 8, LANES), F32),
         pltpu.VMEM((4, 16, LANES), F32),
         pltpu.VMEM((4, 8, LANES), F32),
         pltpu.VMEM((4, 8, LANES), F32),

time: 33.5 us -> 33.2 us (level)
  no operation moved by 1% of the time
where the time goes in v7:
time: 33.2 us; the launch traced here: 33.1 us
  Pallas kernels  31.8 us (96%)
  between operations  1.29 us (4%)
    pallas_call x1, Pallas kernels, on_device(): call(adjoint_start, objective_grad, diagonal, connect, element_scale, ele...  29.4 us
    pallas_call x1, Pallas kernels, finish(): pl.pallas_call(finish_kernel, out_shape=(jax.ShapeDtypeStruct(adjoint.sha...  2.36 us

profile of v7, /device:TPU:1, one launch (start us, length us, event | category | flops | bytes accessed | tf_op | source)
XLA Modules:
  0.0 33.1 jit_solution(8520351346487553493)
XLA Ops:
  1.3 29.4 %shard_map.122 = (f32[6,32,384]{2,1,0:T(8,128)}, f32[128,2,128]{2,1,0:T(2,128)}) custom-call(f32[6,32,384]{2,1,0:T(8,128)} %adj_hbm.1, f32[6,32,384]{2,1,0:T(8,128)} %obj_hbm.1, f32[32,384]{1,0:T(8,128)} %diag_hbm.1, s32[64,338]{1,0:T(8,128)} %conn_hbm.1, f32[64,338]{1,0:T(8,128)} %scale_hbm.1, bf16[64,64]{1,0:T(8,128)(2,1)} %em_hbm.1, f32[3,6]{1,0:T(4,128)} %tm_hbm.1, ...), custom_call_target="tpu_custom_call" | custom-call | tf_op jit(solution)/shard_map/pallas_call | solution.py:671
  30.7 2.4 %shard_map.123 = (f32[6,32,384]{2,1,0:T(8,128)}, f32[3,2,2048]{2,1,0:T(2,128)}) custom-call(f32[6,32,384]{2,1,0:T(8,128)} %get-tuple-element.6.adj, f32[128,2,128]{2,1,0:T(2,128)} %get-tuple-element.7.arr), custom_call_target="tpu_custom_call" | custom-call | tf_op jit(solution)/shard_map/pallas_call | solution.py:733

commit v8 on v7

--- a/solution.py
+++ b/solution.py
@@ -132,6 +132,7 @@
     colhot,
     desthot,
     slot_s,
+    trac_s,
     slothot,
     rowhot,
     names,
@@ -488,8 +489,6 @@
                 p = jnp.where(slots, p.astype(F32), 0.0).astype(BF16)
                 name = name + mm_nt(desthot[:, cols], p)
         names[...] = name
-
-    def tractions(t):
         lane = iota((1, 256), 1)
         trac = []
         for k in range(3):
@@ -497,7 +496,10 @@
             for c in range(COMP):
                 row = jnp.where((lane & 7) == c, tm_ref[k : k + 1, c : c + 1], row)
             trac.append(jnp.where((iota((32, 256), 1) >> 3) == iota((32, 256), 0), row, 0.0))
-        high, low = pieces(jnp.concatenate(trac, axis=0), 2)
+        trac_s[...] = jnp.concatenate(pieces(jnp.concatenate(trac, axis=0), 2), axis=0)
+
+    def tractions(t):
+        high, low = trac_s[0:96], trac_s[96:192]
         own = states[2 * t + 2][UP : UP + ROWS].reshape(ROWS * 8, LANES)
         own_high, own_low = pieces(own, 2)
         field = mm(high, own_high) + (mm(high, own_low) + mm(low, own_high))
@@ -639,6 +641,7 @@
         pltpu.VMEM((LANES, IF_CAP), BF16),
         pltpu.VMEM((D, IF_CAP), BF16),
         pltpu.VMEM((1, IF_CAP), F32),
+        pltpu.VMEM((192, 256), BF16),
         pltpu.VMEM((CAP, IF_CAP), BF16),
         pltpu.VMEM((32, IF_CAP), F32),
         pltpu.VMEM((D, 128), F32),

time: 33.2 us -> 33.2 us (level)
  no operation moved by 1% of the time
where the time goes in v8:
time: 33.2 us; the launch traced here: 33 us
  Pallas kernels  31.7 us (95%)
  between operations  1.29 us (4%)
    pallas_call x1, Pallas kernels, on_device(): call(adjoint_start, objective_grad, diagonal, connect, element_scale, ele...  29.4 us
    pallas_call x1, Pallas kernels, finish(): pl.pallas_call(finish_kernel, out_shape=(jax.ShapeDtypeStruct(adjoint.sha...  2.36 us

profile of v8, /device:TPU:1, one launch (start us, length us, event | category | flops | bytes accessed | tf_op | source)
XLA Modules:
  0.0 33.0 jit_solution(12519769705946002398)
XLA Ops:
  1.3 29.4 %shard_map.122 = (f32[6,32,384]{2,1,0:T(8,128)}, f32[128,2,128]{2,1,0:T(2,128)}) custom-call(f32[6,32,384]{2,1,0:T(8,128)} %adj_hbm.1, f32[6,32,384]{2,1,0:T(8,128)} %obj_hbm.1, f32[32,384]{1,0:T(8,128)} %diag_hbm.1, s32[64,338]{1,0:T(8,128)} %conn_hbm.1, f32[64,338]{1,0:T(8,128)} %scale_hbm.1, bf16[64,64]{1,0:T(8,128)(2,1)} %em_hbm.1, f32[3,6]{1,0:T(4,128)} %tm_hbm.1, ...), custom_call_target="tpu_custom_call" | custom-call | tf_op jit(solution)/shard_map/pallas_call | solution.py:674
  30.6 2.4 %shard_map.123 = (f32[6,32,384]{2,1,0:T(8,128)}, f32[3,2,2048]{2,1,0:T(2,128)}) custom-call(f32[6,32,384]{2,1,0:T(8,128)} %get-tuple-element.6.adj, f32[128,2,128]{2,1,0:T(2,128)} %get-tuple-element.7.arr), custom_call_target="tpu_custom_call" | custom-call | tf_op jit(solution)/shard_map/pallas_call | solution.py:736
